TPU v7x, 128 devices: a whole 4x4x4 slice. The times are simulated.
128 devices in a mesh: blk: 32 (over z_lo, x, y), dp: 4 (over z_hi, core).
Axes of the slice: x: 4, y: 4, z: 4 (z_hi: 2, z_lo: 2; z = z_hi * 2 + z_lo), core: 2. Of those that a mesh axis runs over, the one named last changes fastest.
Arguments:
- segment_sums: bfloat16 [16384, 4096], P(('blk', 'dp')), may hold values from -240 to 240, as said below
- lengths: int32 [16384], P(('blk', 'dp')), may hold values from 8 to 128
- targets: int32 [16384], P(('blk', 'dp')), may hold values from 0 to 16383, as said below
- tile_masks: int32 [128, 2, 2, 2], P(('blk', 'dp')), may hold values from 0 to 1
Outputs:
- pair_losses: float32 [8192], P(('blk', 'dp'))
- sum_gradients: bfloat16 [16384, 4096], P(('blk', 'dp'))
Inputs may be any that keep to these rules, and one draw needn't show every extreme that they name: segment_sums is finite. `targets`: a permutation of the 16384 slots; segment n belongs to owner n // 128 and slot g to loss shard g // 128, both in the order blk then dp; at most 2 segments of one owner go to one loss shard, and every loss shard receives exactly 2 from one owner.
All inputs are finite; a program needn't handle non-finite values.
Results may differ from a plain program's by a relative error of at most 0.0051.
Values may be sent and summed in bfloat16 or wider, within the bound.
A program may use at most 64 MiB of HBM per device.

v0:
```python
import math

import jax
import jax.numpy as jnp
from jax import lax
from jax.sharding import PartitionSpec as P


def from_behind(value, axis, steps):
    count = lax.axis_size(axis)
    pairs = [(source, (source + steps) % count) for source in range(count)]
    return lax.ppermute(value, axis, pairs)


def expand_tiles(tile_bits, tile_rows):
    return jnp.repeat(jnp.repeat(tile_bits, tile_rows, 0), tile_rows, 1) > 0


def tile_product(first_block, second_block, factor):
    return factor * jnp.dot(first_block, second_block.T, preferred_element_type=jnp.float32)


def masked_scores(row_side, column_side, tile_bits, diagonal_on, factor):
    tile_count = tile_bits.shape[0]
    tile_rows = row_side.shape[0] // tile_count
    if diagonal_on:
        tile_bits = jnp.maximum(tile_bits, jnp.eye(tile_count, dtype=jnp.int32))
    products = tile_product(row_side, column_side, factor)
    return jnp.where(expand_tiles(tile_bits, tile_rows), products, -jnp.inf)


def local(segment_sums, lengths, targets, tile_masks):
    blocks = lax.axis_size("blk")
    groups = lax.axis_size("dp")
    devices = blocks * groups
    segment_count = segment_sums.shape[0]
    model_width = segment_sums.shape[1]
    pair_count = segment_count // 2
    capacity = segment_count // devices + max(1, segment_count // (4 * devices))
    factor = 16.0 / math.sqrt(model_width)
    coefficient = factor / (pair_count * devices)
    embedded = (segment_sums.astype(jnp.float32) / lengths.astype(jnp.float32)[:, None]).astype(
        jnp.bfloat16
    )
    owners = targets // segment_count
    within = targets % segment_count
    one_hot = (owners[:, None] == jnp.arange(devices, dtype=jnp.int32)[None, :]).astype(
        jnp.bfloat16
    )
    earlier = (jnp.arange(segment_count)[:, None] > jnp.arange(segment_count)[None, :]).astype(
        jnp.bfloat16
    )
    before = jnp.dot(earlier, one_hot, preferred_element_type=jnp.float32)
    ranking = jnp.sum(before * one_hot.astype(jnp.float32), axis=1).astype(jnp.int32)
    position = owners * capacity + ranking
    send_rows = (
        jnp.zeros((devices * capacity, model_width), jnp.bfloat16).at[position].set(embedded)
    )
    send_slots = jnp.full((devices * capacity,), segment_count, jnp.int32).at[position].set(within)
    send_lengths = jnp.ones((devices * capacity,), jnp.int32).at[position].set(lengths)
    got_rows, got_slots, got_lengths = (
        lax.all_to_all(
            send_rows.reshape(devices, capacity, model_width),
            ("blk", "dp"),
            split_axis=0,
            concat_axis=0,
            tiled=True,
        ),
        lax.all_to_all(
            send_slots.reshape(devices, capacity),
            ("blk", "dp"),
            split_axis=0,
            concat_axis=0,
            tiled=True,
        ),
        lax.all_to_all(
            send_lengths.reshape(devices, capacity),
            ("blk", "dp"),
            split_axis=0,
            concat_axis=0,
            tiled=True,
        ),
    )
    flat_slots = got_slots.reshape(-1)
    placed = (
        jnp.zeros((segment_count, model_width), jnp.bfloat16)
        .at[flat_slots]
        .set(got_rows.reshape(-1, model_width), mode="drop")
    )
    slot_lengths = (
        jnp.ones((segment_count,), jnp.int32)
        .at[flat_slots]
        .set(got_lengths.reshape(-1), mode="drop")
    )
    paired = placed.reshape(pair_count, 2, model_width)
    queries = paired[:, 0]
    documents = paired[:, 1]
    far_documents = from_behind(documents, "blk", 1)
    own_scores = masked_scores(queries, documents, tile_masks[0, 0], True, factor)
    far_scores = masked_scores(queries, far_documents, tile_masks[0, 1], False, factor)
    scores = jnp.concatenate([own_scores, far_scores], 1)
    highest = jnp.max(scores, axis=1, keepdims=True)
    log_total = highest[:, 0] + jnp.log(jnp.sum(jnp.exp(scores - highest), axis=1))
    pair_losses = log_total - jnp.diagonal(own_scores)
    weights = jnp.exp(scores - log_total[:, None]).astype(jnp.bfloat16)
    candidates = jnp.concatenate([documents, far_documents], 0)
    query_gradients = coefficient * (
        jnp.dot(weights, candidates, preferred_element_type=jnp.float32)
        - documents.astype(jnp.float32)
    )
    own_weights = weights[:, :pair_count]
    far_weights = weights[:, pair_count:]
    own_term = jnp.einsum("qp,qw->pw", own_weights, queries, preferred_element_type=jnp.float32)
    document_gradients = coefficient * (own_term - queries.astype(jnp.float32))
    far_term = coefficient * jnp.einsum(
        "qp,qw->pw", far_weights, queries, preferred_element_type=jnp.float32
    )
    document_gradients = document_gradients + from_behind(far_term, "blk", -1)
    slot_gradients = jnp.stack([query_gradients, document_gradients], 1).reshape(
        segment_count, model_width
    )
    slot_gradients = (slot_gradients / slot_lengths.astype(jnp.float32)[:, None]).astype(
        jnp.bfloat16
    )
    returned = jnp.take(slot_gradients, flat_slots, axis=0, mode="clip").reshape(
        devices, capacity, model_width
    )
    arrived = lax.all_to_all(returned, ("blk", "dp"), split_axis=0, concat_axis=0, tiled=True)
    sum_gradients = arrived.reshape(devices * capacity, model_width)[position]
    return (pair_losses, sum_gradients)


def solution(mesh):
    in_specs = (
        P(("blk", "dp"), None),
        P(("blk", "dp")),
        P(("blk", "dp")),
        P(("blk", "dp"), None, None, None),
    )
    out_specs = (P(("blk", "dp")), P(("blk", "dp"), None))
    return jax.shard_map(local, mesh=mesh, in_specs=in_specs, out_specs=out_specs, check_vma=False)
```

profile of v0, /device:TPU:0, one launch (start us, length us, event | category | flops | bytes accessed | tf_op | source)
XLA Modules:
  0.0 172.7 jit_solution(6844988950344584348)
XLA Ops:
  1.5 1.0 scatter_custom_fusion
  3.2 11.1 %all-to-all-start = ((s32[128,1,2]{2,1,0:T(1,128)}), s32[128,1,2]{2,1,0:T(1,128)S(1)}, u32[]{:S(2)}, u32[]{:S(2)}) async-start(s32[128,1,2]{2,1,0:T(1,128)} %bitcast.2), calls=%async_computation | async-start | bytes 131072 | tf_op jit(solution)/shard_map/all_to_all | solution.py:69
  15.1 3.5 %scatter_custom_fusion.1 = bf16[256,4096]{1,0:T(8,128)(2,1)S(1)} fusion(s32[128]{0:T(128)S(1)} %compare_select_fusion.1, bf16[128,4096]{1,0:T(8,128)(2,1)} %param.4, f32[128]{0:T(128)S(1)} %convert_element_type.42, bf16[]{:T(256)} %constant.25.clone.1), kind=kCustom, calls=%fused_computation.25 | custom fusion | flops 1572864 | bytes 3146242 | tf_op jit(solution)/shard_map/scatter | solution.py:57
  18.6 2.7 %reshape.99 = bf16[128,2,4096]{2,1,0:T(2,128)(2,1)} reshape(bf16[256,4096]{1,0:T(8,128)(2,1)S(1)} %scatter_custom_fusion.1) | data formatting | bytes 4194304 | tf_op jit(solution)/shard_map/reshape | solution.py:63
  21.2 2.1 %all-to-all-done = s32[128,1,2]{2,1,0:T(1,128)S(1)} async-done(((s32[128,1,2]{2,1,0:T(1,128)}), s32[128,1,2]{2,1,0:T(1,128)S(1)}, u32[]{:S(2)}, u32[]{:S(2)}) %all-to-all-start) | async-done | bytes 1056 | tf_op jit(solution)/shard_map/all_to_all | solution.py:69
  23.3 7.7 %all-to-all-start.1 = ((bf16[128,2,4096]{2,1,0:T(2,128)(2,1)}), bf16[128,2,4096]{2,1,0:T(2,128)(2,1)S(1)}, u32[]{:S(2)}, u32[]{:S(2)}) async-start(bf16[128,2,4096]{2,1,0:T(2,128)(2,1)} %reshape.99), calls=%async_computation.1 | async-start | bytes 4194304 | tf_op jit(solution)/shard_map/all_to_all | solution.py:62
  32.8 26.6 %all-to-all-done.1 = bf16[128,2,4096]{2,1,0:T(2,128)(2,1)S(1)} async-done(((bf16[128,2,4096]{2,1,0:T(2,128)(2,1)}), bf16[128,2,4096]{2,1,0:T(2,128)(2,1)S(1)}, u32[]{:S(2)}, u32[]{:S(2)}) %all-to-all-start.1) | async-done | bytes 2097184 | tf_op jit(solution)/shard_map/all_to_all | solution.py:62
  59.4 2.2 %reshape.148 = bf16[256,4096]{1,0:T(8,128)(2,1)} reshape(bf16[128,2,4096]{2,1,0:T(2,128)(2,1)S(1)} %all-to-all-done.1) | data formatting | bytes 4194304 | tf_op jit(solution)/shard_map/reshape | solution.py:88
  61.6 4.6 %scatter_custom_fusion.2 = bf16[128,4096]{1,0:T(8,128)(2,1)S(1)} fusion(s32[256]{0:T(256)S(1)} %bitcast.49, bf16[256,4096]{1,0:T(8,128)(2,1)} %reshape.148, bf16[]{:T(256)} %constant.25.clone.1), kind=kCustom, calls=%fused_computation.33 | custom fusion | bytes 1049088 | tf_op jit(solution)/shard_map/scatter | solution.py:88
  67.0 1.5 fusion.30
  69.0 2.1 %collective-permute-start = (bf16[64,4096]{1,0:T(8,128)(2,1)S(1)}, bf16[64,4096]{1,0:T(8,128)(2,1)S(1)}, u32[]{:S(2)}, u32[]{:S(2)}) collective-permute-start(bf16[64,4096]{1,0:T(8,128)(2,1)S(1)} %bitcast.42), channel_id=1, source_target_pairs={{0,4},{4,8},{8,12},{12,16},{16,20},{20,24},{24,28},{28,32},{32,36}... | collective-permute-start | bytes 1572872 | tf_op jit(solution)/shard_map/ppermute | solution.py:12
  73.4 14.8 %collective-permute-done = bf16[64,4096]{1,0:T(8,128)(2,1)S(1)} collective-permute-done((bf16[64,4096]{1,0:T(8,128)(2,1)S(1)}, bf16[64,4096]{1,0:T(8,128)(2,1)S(1)}, u32[]{:S(2)}, u32[]{:S(2)}) %collective-permute-start) | collective-permute-done | bytes 524320 | tf_op jit(solution)/shard_map/ppermute | solution.py:12
  89.9 1.1 scatter_custom_fusion.3
  91.2 24.6 %all_to_all.28 = s32[128,1,2]{2,1,0:T(1,128)S(1)} all-to-all(s32[128,1,2]{2,1,0:T(1,128)S(1)} %bitcast.46), channel_id=1, replica_groups=mesh['blk'=32,'dp'=4] {'blk','dp'}, dimensions={0} | all-to-all | bytes 2048 | tf_op jit(solution)/shard_map/all_to_all | solution.py:76
  116.9 1.4 scatter_custom_fusion.4
  118.7 1.5 fusion.4
  120.4 3.0 %copy.24 = f32[64,2,4096]{2,1,0:T(2,128)} copy(f32[64,2,4096]{2,0,1:T(8,128)S(1)} %pad_maximum_fusion) | data formatting | bytes 4194304 | tf_op jit(solution)/shard_map/stack | solution.py:119
  123.4 2.7 %reshape.102 = f32[128,4096]{1,0:T(8,128)S(1)} reshape(f32[64,2,4096]{2,1,0:T(2,128)} %copy.24) | data formatting | bytes 4194304 | tf_op jit(solution)/shard_map/reshape | solution.py:119
  126.3 1.8 %gather_fusion.1 = bf16[256,4096]{1,0:T(8,128)(2,1)S(1)} fusion(bf16[128,4096]{1,0:T(8,128)(2,1)S(1)} %divide_convert_fusion, s32[1024]{0:T(1024)S(1)} %pad_clamp_fusion.1), kind=kCustom, calls=%fused_computation.1 | custom fusion | bytes 4195328 | tf_op jit(solution)/shard_map/jit(_take)/gather | solution.py:125
  128.2 2.7 %reshape.104 = bf16[128,2,4096]{2,1,0:T(2,128)(2,1)} reshape(bf16[256,4096]{1,0:T(8,128)(2,1)S(1)} %gather_fusion.1) | data formatting | bytes 4194304 | tf_op jit(solution)/shard_map/reshape | solution.py:125
  130.8 9.1 %all-to-all-start.3 = ((bf16[128,2,4096]{2,1,0:T(2,128)(2,1)}), bf16[128,2,4096]{2,1,0:T(2,128)(2,1)}, u32[]{:S(2)}, u32[]{:S(2)}) async-start(bf16[128,2,4096]{2,1,0:T(2,128)(2,1)} %reshape.104), calls=%async_computation.3 | async-start | bytes 4194304 | tf_op jit(solution)/shard_map/all_to_all | solution.py:128
  139.9 27.9 %all-to-all-done.3 = bf16[128,2,4096]{2,1,0:T(2,128)(2,1)} async-done(((bf16[128,2,4096]{2,1,0:T(2,128)(2,1)}), bf16[128,2,4096]{2,1,0:T(2,128)(2,1)}, u32[]{:S(2)}, u32[]{:S(2)}) %all-to-all-start.3) | async-done | bytes 2097184 | tf_op jit(solution)/shard_map/all_to_all | solution.py:128
  167.8 2.7 %reshape.105 = bf16[256,4096]{1,0:T(8,128)(2,1)S(1)} reshape(bf16[128,2,4096]{2,1,0:T(2,128)(2,1)} %all-to-all-done.3) | data formatting | bytes 4194304 | tf_op jit(solution)/shard_map/reshape | solution.py:129
  170.6 2.2 %gather_fusion.2 = bf16[128,4096]{1,0:T(8,128)(2,1)} fusion(bf16[256,4096]{1,0:T(8,128)(2,1)S(1)} %reshape.105, s32[1024]{0:T(1024)S(1)} %pad_clamp_fusion), kind=kCustom, calls=%fused_computation.2 | custom fusion | bytes 2097664 | tf_op jit(solution)/shard_map/gather | solution.py:129
  (47 shorter events, 11.2 us)
Async XLA Ops:
  3.2 20.1 %all-to-all-start = ((s32[128,1,2]{2,1,0:T(1,128)}), s32[128,1,2]{2,1,0:T(1,128)S(1)}, u32[]{:S(2)}, u32[]{:S(2)}) async-start(s32[128,1,2]{2,1,0:T(1,128)} %bitcast.2), calls=%async_computation | async-start | bytes 131072 | tf_op jit(solution)/shard_map/all_to_all | solution.py:69
  21.2 9.8 %copy-start = (s32[1,2,2,2]{3,2,1,0:T(2,128)S(1)}, s32[1,2,2,2]{3,2,1,0:T(2,128)}, u32[]{:S(2)}) copy-start(s32[1,2,2,2]{3,2,1,0:T(2,128)} %param.7) | copy-start | bytes 100
  23.3 36.0 %all-to-all-start.1 = ((bf16[128,2,4096]{2,1,0:T(2,128)(2,1)}), bf16[128,2,4096]{2,1,0:T(2,128)(2,1)S(1)}, u32[]{:S(2)}, u32[]{:S(2)}) async-start(bf16[128,2,4096]{2,1,0:T(2,128)(2,1)} %reshape.99), calls=%async_computation.1 | async-start | bytes 4194304 | tf_op jit(solution)/shard_map/all_to_all | solution.py:62
  69.0 19.2 %collective-permute-start = (bf16[64,4096]{1,0:T(8,128)(2,1)S(1)}, bf16[64,4096]{1,0:T(8,128)(2,1)S(1)}, u32[]{:S(2)}, u32[]{:S(2)}) collective-permute-start(bf16[64,4096]{1,0:T(8,128)(2,1)S(1)} %bitcast.42), channel_id=1, source_target_pairs={{0,4},{4,8},{8,12},{12,16},{16,20},{20,24},{24,28},{28,32},{32,36}... | collective-permute-start | bytes 1572872 | tf_op jit(solution)/shard_map/ppermute | solution.py:12
  89.8 28.8 %collective-permute-start.1 = (f32[64,4096]{1,0:T(8,128)S(1)}, f32[64,4096]{1,0:T(8,128)}, u32[]{:S(2)}, u32[]{:S(2)}) collective-permute-start(f32[64,4096]{1,0:T(8,128)S(1)} %convolution_multiply_fusion), channel_id=1, source_target_pairs={{0,124},{4,0},{8,4},{12,8},{16,12},{20,16},{24,20},{28,24},{32,28}... | collective-permute-start | bytes 3145736 | tf_op jit(solution)/shard_map/ppermute | solution.py:12
  130.8 37.0 %all-to-all-start.3 = ((bf16[128,2,4096]{2,1,0:T(2,128)(2,1)}), bf16[128,2,4096]{2,1,0:T(2,128)(2,1)}, u32[]{:S(2)}, u32[]{:S(2)}) async-start(bf16[128,2,4096]{2,1,0:T(2,128)(2,1)} %reshape.104), calls=%async_computation.3 | async-start | bytes 4194304 | tf_op jit(solution)/shard_map/all_to_all | solution.py:128
where the time goes:
time: 175 us; the launch traced here: 173 us
  waiting for transfers between devices  71.4 us (41%)
  local copies, waits for them, and re-layouts  34.8 us (20%)
  starting transfers between devices  30 us (17%)
  blocking collectives  24.6 us (14%)
  other arithmetic  7.72 us (4%)
  matrix products  3.18 us (2%)
    all_to_all x1, waiting for transfers between devices, local(): lax.all_to_all(returned, ('blk', 'dp'), split_axis=0, concat_axis=0, tile...  27.9 us
    all_to_all x1, waiting for transfers between devices, local(): lax.all_to_all(send_rows.reshape(devices, capacity, model_width), ('blk',...  26.6 us
    all_to_all x1, blocking collectives, local(): lax.all_to_all(send_lengths.reshape(devices, capacity), ('blk', 'dp'), sp...  24.6 us
    ppermute x2, waiting for transfers between devices, from_behind(): return lax.ppermute(value, axis, pairs)  14.8 us
    all_to_all x1, starting transfers between devices, local(): lax.all_to_all(send_slots.reshape(devices, capacity), ('blk', 'dp'), spli...  11.1 us
    all_to_all x1, starting transfers between devices, local(): lax.all_to_all(returned, ('blk', 'dp'), split_axis=0, concat_axis=0, tile...  9.06 us
    all_to_all x1, starting transfers between devices, local(): lax.all_to_all(send_rows.reshape(devices, capacity, model_width), ('blk',...  7.68 us
    scatter x1, local copies, waits for them, and re-layouts, local(): placed = jnp.zeros((segment_count, model_width), jnp.bfloat16).at[flat_sl...  4.64 us
  transfers between devices with their start and end apart: 5, of which 4 were waited for; matrix products, arithmetic and copies ran while one was open for 9% of the time, Pallas kernels for 0%

commit v1 on v0

v1 whole, which is shorter than its diff:
```python
import functools
import math

import jax
import jax.numpy as jnp
from jax import lax
from jax.experimental import pallas as pl
from jax.experimental.pallas import tpu as pltpu
from jax.sharding import PartitionSpec as P

MESH = pl.DeviceIdType.MESH
GROUP = 8
WIDE = 512
RINGS = 16
DEVICES = 128
ROWS = 128
PAIRS = 64
MSG = 16
F32 = jnp.float32
BF16 = jnp.bfloat16


def iota(shape, dim):
    return lax.broadcasted_iota(jnp.int32, shape, dim)


def nt_dot(a, b):
    return lax.dot_general(a, b, (((1,), (1,)), ((), ())), preferred_element_type=F32)


def tn_dot(a, b):
    return lax.dot_general(a, b, (((0,), (0,)), ((), ())), preferred_element_type=F32)


def nn_dot(a, b):
    return jnp.dot(a, b, preferred_element_type=F32)


def one_hot(mask):
    return jnp.where(mask, 1.0, 0.0).astype(BF16)


def place(part, ring):
    return (ring // 4) * 8 + part, ring % 4


def kernel(
    factor,
    coefficient,
    sums_ref,
    lengths_ref,
    targets_ref,
    masks_ref,
    loss_ref,
    out_ref,
    send_one_hot,
    back_one_hot,
    sent,
    landed,
    meta_out,
    meta,
    codes,
    place_one_hot,
    return_one_hot,
    inverse,
    queries,
    documents,
    partial,
    gathered,
    weights,
    totals,
    gradients,
    returning,
    returned,
    send_sem,
    land_sem,
    meta_send_sem,
    meta_sem,
    spread_send_sem,
    spread_sem,
    side_send_sem,
    side_sem,
    score_send_sem,
    score_sem,
    weight_send_sem,
    weight_sem,
    back_send_sem,
    back_sem,
):
    blk = lax.axis_index("blk")
    dp = lax.axis_index("dp")
    part = blk % 8
    ring = (blk // 8) * 4 + dp
    me = part * 16 + ring

    def remote(src, dst, send, recv, to_part, to_ring):
        return pltpu.make_async_remote_copy(
            src_ref=src,
            dst_ref=dst,
            send_sem=send,
            recv_sem=recv,
            device_id=place(to_part, to_ring),
            device_id_type=MESH,
        )

    barrier = pltpu.get_barrier_semaphore()

    def greet(step, carry):
        other = (me + step) % DEVICES
        pl.semaphore_signal(
            barrier, inc=1, device_id=place(other // 16, other % 16), device_id_type=MESH
        )
        return carry

    lax.fori_loop(1, DEVICES, greet, 0)

    target = targets_ref[...]
    length = lengths_ref[...].astype(F32)
    shard = target // ROWS
    slot = target % ROWS
    block = shard // 4
    to_ring = (block // 8) * 4 + shard % 4
    of_shard = one_hot(iota((DEVICES, ROWS), 0) == shard)
    earlier = one_hot(iota((ROWS, ROWS), 0) < iota((ROWS, ROWS), 1))
    before = nn_dot(of_shard, earlier)
    rank = jnp.sum(before * of_shard.astype(F32), axis=0, keepdims=True).astype(jnp.int32)
    inner = (block % 8) * 2 + rank
    position = to_ring * MSG + inner
    send_one_hot[...] = one_hot(iota((2 * ROWS, ROWS), 0) == position)
    column = jnp.transpose(jnp.broadcast_to(position.astype(F32), (ROWS, ROWS))).astype(jnp.int32)
    lanes = iota((ROWS, ROWS), 1)
    back_one_hot[:, :ROWS] = one_hot(column == lanes)
    back_one_hot[:, ROWS:] = one_hot(column == lanes + ROWS)
    code = ((slot % 2) * PAIRS + slot // 2 + 1).astype(F32)
    mine = iota((RINGS, ROWS), 0) == to_ring
    spot = one_hot(iota((ROWS, ROWS), 0) == (ring % 8) * MSG + inner)
    code_rows = nt_dot(jnp.where(mine, code, 0.0).astype(BF16), spot)
    length_rows = nt_dot(jnp.where(mine, length, 0.0).astype(BF16), spot)
    for g in range(RINGS):
        meta_out[g, 0:1, :] = code_rows[g : g + 1]
        meta_out[g, 1:2, :] = length_rows[g : g + 1]
    scale = 1.0 / jnp.transpose(jnp.broadcast_to(length, (ROWS, ROWS)))
    scale = jnp.concatenate([scale] * (WIDE // ROWS), axis=1)

    def pack(step, carry):
        k = (part + step) % GROUP
        columns = sums_ref[:, pl.ds(pl.multiple_of(k * WIDE, WIDE), WIDE)].astype(F32)
        embedded = (columns * scale).astype(BF16)
        sent[k] = nn_dot(send_one_hot[...], embedded).astype(BF16)
        return carry

    lax.fori_loop(0, GROUP, pack, 0)

    pl.semaphore_wait(barrier, DEVICES - 1)

    def meta_hop(step, carry):
        g = (ring + step) % RINGS
        src, dst = meta_out.at[g], meta.at[ring % 8, part * 2 + ring // 8]

        @pl.when((g == ring) & (part == ring % 8))
        def _():
            pltpu.make_async_copy(src, dst, meta_sem).start()

        @pl.when(jnp.logical_not((g == ring) & (part == ring % 8)))
        def _():
            remote(src, dst, meta_send_sem, meta_sem, ring % 8, g).start()

        return carry

    lax.fori_loop(0, RINGS, meta_hop, 0)

    def rows_out(step, carry):
        k = (part + step // RINGS) % GROUP
        g = (ring + step % RINGS) % RINGS
        src = sent.at[k, pl.ds(pl.multiple_of(g * MSG, MSG), MSG)]
        dst = landed.at[pl.ds(pl.multiple_of(me * MSG, MSG), MSG)]
        remote(src, dst, send_sem, land_sem.at[part], k, g).start()
        return carry

    pltpu.make_async_copy(
        sent.at[part, pl.ds(pl.multiple_of(ring * MSG, MSG), MSG)],
        landed.at[pl.ds(pl.multiple_of(me * MSG, MSG), MSG)],
        land_sem.at[part],
    ).start()
    lax.fori_loop(1, DEVICES, rows_out, 0)

    pltpu.make_async_copy(meta.at[part], meta.at[part], meta_sem).wait()

    def spread(step, carry):
        k = (part + step) % GROUP
        remote(
            meta.at[part], meta.at[part], spread_send_sem.at[step], spread_sem.at[part], k, ring
        ).start()
        return carry

    lax.fori_loop(1, GROUP, spread, 0)

    def spread_wait(step, carry):
        k = (part + GROUP - step) % GROUP
        remote(
            meta.at[k], meta.at[k], spread_send_sem.at[step], spread_sem.at[k], k, ring
        ).wait_recv()
        return carry

    lax.fori_loop(1, GROUP, spread_wait, 0)
    both = meta[0]
    for k in range(1, GROUP):
        both = both + meta[k]
    codes[...] = both

    inner_shard = (iota((1, ROWS), 1) % MSG) // 2

    def build(a, total):
        pair = codes[a]
        raw = pair[0:1].astype(jnp.int32) - 1
        live = jnp.where(raw >= PAIRS, 7 * PAIRS + raw, raw) + inner_shard * PAIRS
        full = jnp.where(raw >= 0, live, -1)
        matrix = one_hot(iota((8 * ROWS, ROWS), 0) == full)
        place_one_hot[a] = matrix
        down = jnp.transpose(jnp.broadcast_to(full.astype(F32), (ROWS, ROWS))).astype(jnp.int32)
        for s in range(GROUP):
            return_one_hot[pl.ds(pl.multiple_of(a * ROWS, ROWS), ROWS), s * ROWS : (s + 1) * ROWS] = (
                one_hot(down == lanes + s * ROWS)
            )
        wide = jnp.broadcast_to(pair[1:2], (ROWS, ROWS)).astype(BF16)
        inverse[...] = jnp.where(a == 0, 0.0, inverse[...]) + nt_dot(matrix, wide)
        return total

    inverse[...] = jnp.zeros(inverse.shape, F32)
    lax.fori_loop(0, 16, build, 0)
    inverse[...] = coefficient / inverse[...]

    def rows_wait(step, carry):
        k = (part + GROUP - step) % GROUP
        chunk = landed.at[pl.ds(pl.multiple_of(k * 256, 256), 256)]
        pltpu.make_async_copy(chunk, chunk, land_sem.at[k]).wait()
        return carry

    lax.fori_loop(0, GROUP, rows_wait, 0)

    def put(half):
        matrix = jnp.concatenate(
            [place_one_hot[a, half * 512 : (half + 1) * 512] for a in range(16)], axis=1
        )
        return nn_dot(matrix, landed[...]).astype(BF16)

    documents[PAIRS:] = put(1)
    queries[: 8 * PAIRS] = put(0)

    after = (ring + 4) % RINGS
    ahead = (ring + 12) % RINGS
    to_next = remote(
        documents.at[8 * PAIRS :], documents.at[:PAIRS], side_send_sem.at[0], side_sem.at[0], part, after
    )
    to_last = remote(
        queries.at[:PAIRS], queries.at[8 * PAIRS :], side_send_sem.at[1], side_sem.at[1], part, ahead
    )
    to_next.start()
    to_last.start()

    to_next.wait_recv()

    def score(step, carry):
        s = (part + step) % GROUP
        rows = queries[pl.ds(pl.multiple_of(s * PAIRS, PAIRS), PAIRS)]
        others = documents[pl.ds(pl.multiple_of(s * PAIRS, PAIRS), 2 * PAIRS)]
        partial[s] = nt_dot(rows, others)
        remote(
            partial.at[s], gathered.at[part], score_send_sem.at[step], score_sem.at[part], s, ring
        ).start()
        return carry

    lax.fori_loop(1, GROUP, score, 0)
    own_rows = queries[pl.ds(pl.multiple_of(part * PAIRS, PAIRS), PAIRS)]
    own_others = documents[pl.ds(pl.multiple_of(part * PAIRS, PAIRS), 2 * PAIRS)]
    gathered[part] = nt_dot(own_rows, own_others)

    def score_wait(step, carry):
        k = (part + GROUP - step) % GROUP
        remote(
            partial.at[k], gathered.at[k], score_send_sem.at[step], score_sem.at[k], k, ring
        ).wait_recv()
        return carry

    lax.fori_loop(1, GROUP, score_wait, 0)
    scores = gathered[0]
    for k in range(1, GROUP):
        scores = scores + gathered[k]
    scores = factor * scores

    row = iota((PAIRS, 2 * PAIRS), 0)
    col = iota((PAIRS, 2 * PAIRS), 1)

    def tile(stop, i, j):
        return masks_ref[stop * 4 + i * 2 + j]

    top = jnp.where(
        col < 32,
        tile(1, 0, 0),
        jnp.where(col < 64, tile(1, 0, 1), jnp.where(col < 96, 1, tile(0, 0, 1))),
    )
    low = jnp.where(
        col < 32,
        tile(1, 1, 0),
        jnp.where(col < 64, tile(1, 1, 1), jnp.where(col < 96, tile(0, 1, 0), 1)),
    )
    live = jnp.where(row < 32, top, low) > 0
    masked = jnp.where(live, scores, -jnp.inf)
    highest = jnp.max(masked, axis=1, keepdims=True)
    log_total = highest + jnp.log(jnp.sum(jnp.exp(masked - highest), axis=1, keepdims=True))
    diagonal = jnp.sum(jnp.where(col == row + PAIRS, scores, 0.0), axis=1, keepdims=True)
    losses = jnp.where(col == row, log_total - diagonal, 0.0)
    loss_ref[...] = jnp.sum(losses, axis=0, keepdims=True)[:, :PAIRS]
    weights[part] = jnp.exp(masked - log_total).astype(BF16)

    def weight_out(step, carry):
        s = (part + step) % GROUP
        remote(
            weights.at[part], weights.at[part], weight_send_sem.at[step], weight_sem.at[part], s, ring
        ).start()
        return carry

    lax.fori_loop(1, GROUP, weight_out, 0)

    @pl.when(part == 0)
    def _():
        def far_out(step, carry):
            remote(
                weights.at[0], weights.at[8], weight_send_sem.at[8 + step], weight_sem.at[8], step, ahead
            ).start()
            return carry

        lax.fori_loop(0, GROUP, far_out, 0)

    def weight_wait(step, carry):
        k = (part + GROUP - step) % GROUP
        remote(
            weights.at[k], weights.at[k], weight_send_sem.at[step], weight_sem.at[k], k, ring
        ).wait_recv()
        return carry

    lax.fori_loop(1, GROUP, weight_wait, 0)
    remote(weights.at[0], weights.at[8], weight_send_sem.at[8], weight_sem.at[8], 0, ahead).wait_recv()
    to_last.wait_recv()

    def spread_scale(value):
        return jnp.concatenate([value] * (WIDE // ROWS), axis=1)

    def gradient(s, carry):
        start = pl.multiple_of(s * PAIRS, PAIRS)
        one = pl.ds(start, PAIRS)
        after_one = pl.ds(pl.multiple_of(s * PAIRS + PAIRS, PAIRS), PAIRS)
        two = pl.ds(start, 2 * PAIRS)
        weight = weights[s]
        term = nn_dot(weight, documents[two]) - documents[after_one].astype(F32)
        gradients[one] = (term * spread_scale(inverse[one])).astype(BF16)
        far = tn_dot(weight, queries[one])
        totals[one] = totals[one] + far[:PAIRS]
        totals[after_one] = far[PAIRS:] - queries[one].astype(F32)
        return carry

    totals[:PAIRS] = jnp.zeros((PAIRS, WIDE), F32)
    lax.fori_loop(0, GROUP, gradient, 0)
    totals[8 * PAIRS :] = totals[8 * PAIRS :] + tn_dot(weights[8], queries[8 * PAIRS :])[:PAIRS]
    gradients[8 * PAIRS :] = (totals[PAIRS:] * spread_scale(inverse[8 * PAIRS :])).astype(BF16)

    def rows_back(step, carry):
        k = (part + step) % GROUP
        rows = pl.ds(pl.multiple_of(k * 256, 256), 256)
        returning[rows] = nn_dot(return_one_hot[rows], gradients[...]).astype(BF16)

        def one(turn, inner_carry):
            g = (ring + turn) % RINGS
            src = returning.at[pl.ds(pl.multiple_of((k * 16 + g) * MSG, MSG), MSG)]
            dst = returned.at[part, pl.ds(pl.multiple_of(ring * MSG, MSG), MSG)]
            remote(src, dst, back_send_sem, back_sem.at[part], k, g).start()
            return inner_carry

        @pl.when(step == 0)
        def _():
            pltpu.make_async_copy(
                returning.at[pl.ds(pl.multiple_of(me * MSG, MSG), MSG)],
                returned.at[part, pl.ds(pl.multiple_of(ring * MSG, MSG), MSG)],
                back_sem.at[part],
            ).start()

        lax.fori_loop(jnp.where(step == 0, 1, 0), RINGS, one, 0)
        return carry

    lax.fori_loop(0, GROUP, rows_back, 0)

    def finish(step, carry):
        k = (part + GROUP - step) % GROUP
        pltpu.make_async_copy(returned.at[k], returned.at[k], back_sem.at[k]).wait()
        out_ref[:, pl.ds(pl.multiple_of(k * WIDE, WIDE), WIDE)] = nn_dot(
            back_one_hot[...], returned[k]
        ).astype(BF16)
        return carry

    lax.fori_loop(0, GROUP, finish, 0)

    most = landed.at[pl.ds(0, (DEVICES - 1) * MSG)]
    pltpu.make_async_copy(most, most, send_sem).wait()
    pltpu.make_async_copy(most, most, back_send_sem).wait()

    @pl.when(part == ring % 8)
    def _():
        fifteen = meta_out.at[pl.ds(0, RINGS - 1)]
        pltpu.make_async_copy(fifteen, fifteen, meta_send_sem).wait()

    @pl.when(part != ring % 8)
    def _():
        pltpu.make_async_copy(meta_out, meta_out, meta_send_sem).wait()

    to_next.wait_send()
    to_last.wait_send()

    def sent_wait(step, carry):
        k = (part + step) % GROUP
        remote(
            meta.at[part], meta.at[part], spread_send_sem.at[step], spread_sem.at[part], k, ring
        ).wait_send()
        remote(
            partial.at[k], gathered.at[part], score_send_sem.at[step], score_sem.at[part], k, ring
        ).wait_send()
        remote(
            weights.at[part], weights.at[part], weight_send_sem.at[step], weight_sem.at[part], k, ring
        ).wait_send()
        return carry

    lax.fori_loop(1, GROUP, sent_wait, 0)

    @pl.when(part == 0)
    def _():
        def far_wait(step, carry):
            remote(
                weights.at[0], weights.at[8], weight_send_sem.at[8 + step], weight_sem.at[8], step, ahead
            ).wait_send()
            return carry

        lax.fori_loop(0, GROUP, far_wait, 0)


def local(segment_sums, lengths, targets, tile_masks):
    width = segment_sums.shape[1]
    factor = 16.0 / math.sqrt(width)
    coefficient = factor / (PAIRS * DEVICES)
    vmem = pl.BlockSpec(memory_space=pltpu.VMEM)
    smem = pl.BlockSpec(memory_space=pltpu.SMEM)
    dma = pltpu.SemaphoreType.DMA
    losses, gradients = pl.pallas_call(
        functools.partial(kernel, factor, coefficient),
        out_shape=(
            jax.ShapeDtypeStruct((1, PAIRS), F32),
            jax.ShapeDtypeStruct((ROWS, width), BF16),
        ),
        in_specs=[vmem, vmem, vmem, smem],
        out_specs=(vmem, vmem),
        scratch_shapes=[
            pltpu.VMEM((2 * ROWS, ROWS), BF16),
            pltpu.VMEM((ROWS, 2 * ROWS), BF16),
            pltpu.VMEM((GROUP, 2 * ROWS, WIDE), BF16),
            pltpu.VMEM((DEVICES * MSG, WIDE), BF16),
            pltpu.VMEM((RINGS, 2, ROWS), F32),
            pltpu.VMEM((GROUP, 16, 2, ROWS), F32),
            pltpu.VMEM((16, 2, ROWS), F32),
            pltpu.VMEM((16, GROUP * ROWS, ROWS), BF16),
            pltpu.VMEM((DEVICES * MSG, GROUP * ROWS), BF16),
            pltpu.VMEM((GROUP * ROWS, ROWS), F32),
            pltpu.VMEM((9 * PAIRS, WIDE), BF16),
            pltpu.VMEM((9 * PAIRS, WIDE), BF16),
            pltpu.VMEM((GROUP, PAIRS, 2 * PAIRS), F32),
            pltpu.VMEM((GROUP, PAIRS, 2 * PAIRS), F32),
            pltpu.VMEM((9, PAIRS, 2 * PAIRS), BF16),
            pltpu.VMEM((9 * PAIRS, WIDE), F32),
            pltpu.VMEM((16 * PAIRS, WIDE), BF16),
            pltpu.VMEM((DEVICES * MSG, WIDE), BF16),
            pltpu.VMEM((GROUP, 2 * ROWS, WIDE), BF16),
            dma,
            dma((GROUP,)),
            dma,
            dma,
            dma((GROUP,)),
            dma((GROUP,)),
            dma((2,)),
            dma((2,)),
            dma((GROUP,)),
            dma((GROUP,)),
            dma((2 * GROUP,)),
            dma((GROUP + 1,)),
            dma,
            dma((GROUP,)),
        ],
        compiler_params=pltpu.CompilerParams(
            collective_id=0, has_side_effects=True, vmem_limit_bytes=56 << 20
        ),
    )(segment_sums, lengths.reshape(1, ROWS), targets.reshape(1, ROWS), tile_masks.reshape(8))
    return losses.reshape(PAIRS), gradients


def solution(mesh):
    in_specs = (
        P(("blk", "dp"), None),
        P(("blk", "dp")),
        P(("blk", "dp")),
        P(("blk", "dp"), None, None, None),
    )
    out_specs = (P(("blk", "dp")), P(("blk", "dp"), None))
    return jax.shard_map(local, mesh=mesh, in_specs=in_specs, out_specs=out_specs, check_vma=False)
```

time: 175 us -> 107 us (0.61)
  Pallas kernels: 0 us -> 101 us
  waiting for transfers between devices: 71.4 us -> 0 us
  local copies, waits for them, and re-layouts: 34.8 us -> 4.72 us
  starting transfers between devices: 30 us -> 0 us
  blocking collectives: 24.6 us -> 0 us
  other arithmetic: 7.72 us -> 0 us
  matrix products: 3.18 us -> 0 us
    pallas_call x0 -> x1, Pallas kernels: none -> 101 us  [local(): pl.pallas_call(functools.partial(kernel, factor, coefficient), out_shape=...]
    all_to_all x3 -> x0, waiting for transfers between devices: 56.6 us -> none  [the longest x1 27.9 us: local(): lax.all_to_all(returned, ('blk', 'dp'), split_axis=0, concat_axis=0, tile...]
    all_to_all x3 -> x0, starting transfers between devices: 27.9 us -> none  [the longest x1 11.1 us: local(): lax.all_to_all(send_slots.reshape(devices, capacity), ('blk', 'dp'), spli...]
    all_to_all x1 -> x0, blocking collectives: 24.6 us -> none  [local(): lax.all_to_all(send_lengths.reshape(devices, capacity), ('blk', 'dp'), sp...]
    ppermute x2 -> x0, waiting for transfers between devices: 14.8 us -> none  [from_behind(): return lax.ppermute(value, axis, pairs)]
    reshape x9 -> x1, local copies, waits for them, and re-layouts: 14.1 us -> 0.59 us  [local(): tile_masks.reshape(8)]
    scatter x4 -> x0, local copies, waits for them, and re-layouts: 8.13 us -> none  [the longest x1 4.64 us: local(): placed = jnp.zeros((segment_count, model_width), jnp.bfloat16).at[flat_sl...]
    gather x3 -> x0, local copies, waits for them, and re-layouts: 4.83 us -> none  [the longest x1 2.16 us: local(): sum_gradients = arrived.reshape(devices * capacity, model_width)[position]]
  transfers between devices with their start and end apart: 5 -> 0, of which waited for: 4 -> 0; matrix products, arithmetic and copies ran while one was open for 9% -> 0% of each run, Pallas kernels for 0% -> 0%
where the time goes in v1:
time: 107 us; the launch traced here: 106 us
  Pallas kernels  101 us (94%)
  local copies, waits for them, and re-layouts  4.72 us (4%)
    pallas_call x1, Pallas kernels, local(): pl.pallas_call(functools.partial(kernel, factor, coefficient), out_shape=...  101 us
    unnamed x6, local copies, waits for them, and re-layouts  4.13 us

profile of v1, /device:TPU:0, one launch (start us, length us, event | category | flops | bytes accessed | tf_op | source)
XLA Modules:
  0.0 106.0 jit_solution(3077961497756653009)
XLA Ops:
  0.6 0.0 copy-start
  0.6 0.7 copy-done
  1.3 0.6 reshape.18.masks_ref
  1.9 100.6 %shard_map.59 = (f32[1,64]{1,0:T(1,128)}, bf16[128,4096]{1,0:T(8,128)(2,1)}) custom-call(bf16[128,4096]{1,0:T(8,128)(2,1)} %sums_ref.1, s32[1,128]{1,0:T(1,128)} %bitcast.3, s32[1,128]{1,0:T(1,128)} %bitcast.4, s32[8]{0:T(128)} %reshape.18.masks_ref), custom_call_target="tpu_custom_call" | custom-call | tf_op jit(solution)/shard_map/pallas_call | solution.py:451
  102.5 0.0 copy-start.1
  102.5 0.7 copy-done.1
  103.2 0.5 copy.8
  103.7 2.3 %copy.9 = bf16[128,4096]{1,0:T(8,128)(2,1)} copy(bf16[128,4096]{1,0:T(8,128)(2,1)} %get-tuple-element.9) | data formatting | bytes 2097152
Async XLA Ops:
  0.6 0.7 copy-start
  102.5 0.7 copy-start.1

commit v2 on v1

--- a/solution.py
+++ b/solution.py
@@ -47,14 +47,15 @@
 def kernel(
     factor,
     coefficient,
-    sums_ref,
+    sums_hbm,
     lengths_ref,
     targets_ref,
     masks_ref,
     loss_ref,
-    out_ref,
+    returned,
+    back_one_hot,
+    sums_ref,
     send_one_hot,
-    back_one_hot,
     sent,
     landed,
     meta_out,
@@ -63,6 +64,7 @@
     place_one_hot,
     return_one_hot,
     inverse,
+    placed,
     queries,
     documents,
     partial,
@@ -71,7 +73,7 @@
     totals,
     gradients,
     returning,
-    returned,
+    load_sem,
     send_sem,
     land_sem,
     meta_send_sem,
@@ -89,9 +91,25 @@
 ):
     blk = lax.axis_index("blk")
     dp = lax.axis_index("dp")
-    part = blk % 8
+    part = lax.rem(blk, 8)
     ring = (blk // 8) * 4 + dp
-    me = part * 16 + ring
+    x, y = lax.rem(blk, 16) // 4, lax.rem(blk, 4)
+    z, core = (dp // 2) * 2 + blk // 16, lax.rem(dp, 2)
+    own_sum = lax.rem(x + y + z, 4)
+    me = (own_sum * 2 + core) * 16 + x * 4 + y
+    xs = [lax.rem(x + i, 4) for i in range(4)]
+    ys = [lax.rem(y + j, 4) for j in range(4)]
+
+    def class_peers(turn, to_core):
+        zs = [lax.rem(z + turn + 4 - m, 4) for m in range(4)]
+        zs = [lax.rem(v, 2) * 8 + (v // 2) * 2 + to_core for v in zs]
+        for i in range(4):
+            for j in range(4):
+                yield (
+                    lax.rem(xs[i], 2) * 4 + ys[j],
+                    (xs[i] // 2) * 4 + zs[(i + j) % 4],
+                    xs[i] * 4 + ys[j],
+                )
 
     def remote(src, dst, send, recv, to_part, to_ring):
         return pltpu.make_async_remote_copy(
@@ -105,14 +123,21 @@
 
     barrier = pltpu.get_barrier_semaphore()
 
-    def greet(step, carry):
-        other = (me + step) % DEVICES
-        pl.semaphore_signal(
-            barrier, inc=1, device_id=place(other // 16, other % 16), device_id_type=MESH
-        )
-        return carry
-
-    lax.fori_loop(1, DEVICES, greet, 0)
+    load = pltpu.make_async_copy(sums_hbm, sums_ref, load_sem)
+    load.start()
+
+    def greet(k, g):
+        pl.semaphore_signal(barrier, inc=1, device_id=place(k, g), device_id_type=MESH)
+
+    def greet_part(step, carry):
+        k = lax.rem(part + step, GROUP)
+        for g in range(RINGS):
+            greet(k, g)
+        return carry
+
+    for turn in range(1, RINGS):
+        greet(part, lax.rem(ring + turn, RINGS))
+    lax.fori_loop(1, GROUP, greet_part, 0)
 
     target = targets_ref[...]
     length = lengths_ref[...].astype(F32)
@@ -133,7 +158,7 @@
     back_one_hot[:, ROWS:] = one_hot(column == lanes + ROWS)
     code = ((slot % 2) * PAIRS + slot // 2 + 1).astype(F32)
     mine = iota((RINGS, ROWS), 0) == to_ring
-    spot = one_hot(iota((ROWS, ROWS), 0) == (ring % 8) * MSG + inner)
+    spot = one_hot(iota((ROWS, ROWS), 0) == part * MSG + inner)
     code_rows = nt_dot(jnp.where(mine, code, 0.0).astype(BF16), spot)
     length_rows = nt_dot(jnp.where(mine, length, 0.0).astype(BF16), spot)
     for g in range(RINGS):
@@ -142,47 +167,49 @@
     scale = 1.0 / jnp.transpose(jnp.broadcast_to(length, (ROWS, ROWS)))
     scale = jnp.concatenate([scale] * (WIDE // ROWS), axis=1)
 
-    def pack(step, carry):
-        k = (part + step) % GROUP
-        columns = sums_ref[:, pl.ds(pl.multiple_of(k * WIDE, WIDE), WIDE)].astype(F32)
+    def pack(k):
+        columns = sums_ref[:, k * WIDE : (k + 1) * WIDE].astype(F32)
         embedded = (columns * scale).astype(BF16)
         sent[k] = nn_dot(send_one_hot[...], embedded).astype(BF16)
-        return carry
-
-    lax.fori_loop(0, GROUP, pack, 0)
+
+    load.wait()
+    for k in range(GROUP):
+        pack(k)
 
     pl.semaphore_wait(barrier, DEVICES - 1)
 
-    def meta_hop(step, carry):
-        g = (ring + step) % RINGS
-        src, dst = meta_out.at[g], meta.at[ring % 8, part * 2 + ring // 8]
-
-        @pl.when((g == ring) & (part == ring % 8))
-        def _():
-            pltpu.make_async_copy(src, dst, meta_sem).start()
-
-        @pl.when(jnp.logical_not((g == ring) & (part == ring % 8)))
-        def _():
-            remote(src, dst, meta_send_sem, meta_sem, ring % 8, g).start()
-
-        return carry
-
-    lax.fori_loop(0, RINGS, meta_hop, 0)
+    meta_dst = meta.at[part, me // 8]
+    pltpu.make_async_copy(meta_out.at[ring], meta_dst, meta_sem).start()
+    for turn in range(1, RINGS):
+        g = lax.rem(ring + turn, RINGS)
+        remote(meta_out.at[g], meta_dst, meta_send_sem, meta_sem, part, g).start()
+
+    land_dst = landed.at[pl.ds(pl.multiple_of(me * MSG, MSG), MSG)]
+
+    own_class = own_sum * 2 + core
+
+    def sent_rows(k, g):
+        return sent.at[k, pl.ds(pl.multiple_of(g * MSG, MSG), MSG)]
 
     def rows_out(step, carry):
-        k = (part + step // RINGS) % GROUP
-        g = (ring + step % RINGS) % RINGS
-        src = sent.at[k, pl.ds(pl.multiple_of(g * MSG, MSG), MSG)]
-        dst = landed.at[pl.ds(pl.multiple_of(me * MSG, MSG), MSG)]
-        remote(src, dst, send_sem, land_sem.at[part], k, g).start()
-        return carry
-
-    pltpu.make_async_copy(
-        sent.at[part, pl.ds(pl.multiple_of(ring * MSG, MSG), MSG)],
-        landed.at[pl.ds(pl.multiple_of(me * MSG, MSG), MSG)],
-        land_sem.at[part],
-    ).start()
-    lax.fori_loop(1, DEVICES, rows_out, 0)
+        turn, to_core = lax.rem(step, 4), step // 4
+        for index, (k, g, _) in enumerate(class_peers(turn, to_core)):
+            if index == 0:
+                stays = (turn == 0) & (to_core == core)
+
+                @pl.when(stays)
+                def _():
+                    pltpu.make_async_copy(sent_rows(k, g), land_dst, land_sem.at[own_class]).start()
+
+                @pl.when(jnp.logical_not(stays))
+                def _():
+                    remote(sent_rows(k, g), land_dst, send_sem, land_sem.at[own_class], k, g).start()
+
+            else:
+                remote(sent_rows(k, g), land_dst, send_sem, land_sem.at[own_class], k, g).start()
+        return carry
+
+    rows_out(0, 0)
 
     pltpu.make_async_copy(meta.at[part], meta.at[part], meta_sem).wait()
 
@@ -194,6 +221,8 @@
         return carry
 
     lax.fori_loop(1, GROUP, spread, 0)
+
+    lax.fori_loop(1, 8, rows_out, 0)
 
     def spread_wait(step, carry):
         k = (part + GROUP - step) % GROUP
@@ -230,23 +259,6 @@
     lax.fori_loop(0, 16, build, 0)
     inverse[...] = coefficient / inverse[...]
 
-    def rows_wait(step, carry):
-        k = (part + GROUP - step) % GROUP
-        chunk = landed.at[pl.ds(pl.multiple_of(k * 256, 256), 256)]
-        pltpu.make_async_copy(chunk, chunk, land_sem.at[k]).wait()
-        return carry
-
-    lax.fori_loop(0, GROUP, rows_wait, 0)
-
-    def put(half):
-        matrix = jnp.concatenate(
-            [place_one_hot[a, half * 512 : (half + 1) * 512] for a in range(16)], axis=1
-        )
-        return nn_dot(matrix, landed[...]).astype(BF16)
-
-    documents[PAIRS:] = put(1)
-    queries[: 8 * PAIRS] = put(0)
-
     after = (ring + 4) % RINGS
     ahead = (ring + 12) % RINGS
     to_next = remote(
@@ -255,30 +267,63 @@
     to_last = remote(
         queries.at[:PAIRS], queries.at[8 * PAIRS :], side_send_sem.at[1], side_sem.at[1], part, ahead
     )
+
+    def land(step):
+        k = lax.rem(own_sum + 4 - step // 2, 4) * 2 + lax.rem(step, 2)
+        rows = pl.ds(pl.multiple_of(k * 256, 256), 256)
+        pltpu.make_async_copy(landed.at[rows], landed.at[rows], land_sem.at[k]).wait()
+        return k, rows
+
+    def put(step, block):
+        k, rows = step
+        slots = pl.ds(block * 256, 256)
+        matrix = jnp.concatenate([place_one_hot[2 * k, slots], place_one_hot[2 * k + 1, slots]], axis=1)
+        return nn_dot(matrix, landed[rows])
+
+    def put_all(step, carry):
+        now = land(step)
+        for block in range(4):
+            slots = pl.ds(block * 256, 256)
+            placed[slots] = jnp.where(step == 0, 0.0, placed[slots]) + put(now, block)
+        return carry
+
+    placed[...] = jnp.zeros(placed.shape, F32)
+    lax.fori_loop(0, GROUP - 1, put_all, 0)
+    last = land(GROUP - 1)
+    documents[320:576] = (placed[768:1024] + put(last, 3)).astype(BF16)
     to_next.start()
+    queries[0:256] = (placed[0:256] + put(last, 0)).astype(BF16)
     to_last.start()
-
+    queries[256:512] = (placed[256:512] + put(last, 1)).astype(BF16)
+    documents[64:320] = (placed[512:768] + put(last, 2)).astype(BF16)
+
+    def score(s):
+        start = pl.multiple_of(s * PAIRS, PAIRS)
+        value = nt_dot(queries[pl.ds(start, PAIRS)], documents[pl.ds(start, 2 * PAIRS)])
+
+        @pl.when(s == part)
+        def _():
+            gathered[part] = value
+
+        @pl.when(s != part)
+        def _():
+            partial[s] = value
+            remote(
+                partial.at[s], gathered.at[part], score_send_sem.at[s], score_sem.at[part], s, ring
+            ).start()
+
+    def score_step(step, carry):
+        score(1 + lax.rem(part + step, GROUP - 1))
+        return carry
+
+    lax.fori_loop(0, GROUP - 1, score_step, 0)
     to_next.wait_recv()
-
-    def score(step, carry):
-        s = (part + step) % GROUP
-        rows = queries[pl.ds(pl.multiple_of(s * PAIRS, PAIRS), PAIRS)]
-        others = documents[pl.ds(pl.multiple_of(s * PAIRS, PAIRS), 2 * PAIRS)]
-        partial[s] = nt_dot(rows, others)
-        remote(
-            partial.at[s], gathered.at[part], score_send_sem.at[step], score_sem.at[part], s, ring
-        ).start()
-        return carry
-
-    lax.fori_loop(1, GROUP, score, 0)
-    own_rows = queries[pl.ds(pl.multiple_of(part * PAIRS, PAIRS), PAIRS)]
-    own_others = documents[pl.ds(pl.multiple_of(part * PAIRS, PAIRS), 2 * PAIRS)]
-    gathered[part] = nt_dot(own_rows, own_others)
+    score(0)
 
     def score_wait(step, carry):
         k = (part + GROUP - step) % GROUP
         remote(
-            partial.at[k], gathered.at[k], score_send_sem.at[step], score_sem.at[k], k, ring
+            partial.at[k], gathered.at[k], score_send_sem.at[k], score_sem.at[k], k, ring
         ).wait_recv()
         return carry
 
@@ -292,7 +337,7 @@
     col = iota((PAIRS, 2 * PAIRS), 1)
 
     def tile(stop, i, j):
-        return masks_ref[stop * 4 + i * 2 + j]
+        return masks_ref[0, stop, i, j]
 
     top = jnp.where(
         col < 32,
@@ -364,37 +409,38 @@
     totals[8 * PAIRS :] = totals[8 * PAIRS :] + tn_dot(weights[8], queries[8 * PAIRS :])[:PAIRS]
     gradients[8 * PAIRS :] = (totals[PAIRS:] * spread_scale(inverse[8 * PAIRS :])).astype(BF16)
 
+    back_dst = returned.at[part, pl.ds(pl.multiple_of(ring * MSG, MSG), MSG)]
+
+    def back_rows(label, spot):
+        return returning.at[pl.ds(pl.multiple_of((label * 16 + spot) * MSG, MSG), MSG)]
+
     def rows_back(step, carry):
-        k = (part + step) % GROUP
-        rows = pl.ds(pl.multiple_of(k * 256, 256), 256)
+        turn, to_core = lax.rem(step, 4), step // 4
+        label = lax.rem(own_sum + turn, 4) * 2 + to_core
+        rows = pl.ds(pl.multiple_of(label * 256, 256), 256)
         returning[rows] = nn_dot(return_one_hot[rows], gradients[...]).astype(BF16)
-
-        def one(turn, inner_carry):
-            g = (ring + turn) % RINGS
-            src = returning.at[pl.ds(pl.multiple_of((k * 16 + g) * MSG, MSG), MSG)]
-            dst = returned.at[part, pl.ds(pl.multiple_of(ring * MSG, MSG), MSG)]
-            remote(src, dst, back_send_sem, back_sem.at[part], k, g).start()
-            return inner_carry
-
-        @pl.when(step == 0)
-        def _():
-            pltpu.make_async_copy(
-                returning.at[pl.ds(pl.multiple_of(me * MSG, MSG), MSG)],
-                returned.at[part, pl.ds(pl.multiple_of(ring * MSG, MSG), MSG)],
-                back_sem.at[part],
-            ).start()
-
-        lax.fori_loop(jnp.where(step == 0, 1, 0), RINGS, one, 0)
-        return carry
-
-    lax.fori_loop(0, GROUP, rows_back, 0)
+        for index, (k, g, spot) in enumerate(class_peers(turn, to_core)):
+            src = back_rows(label, spot)
+            if index == 0:
+                stays = (turn == 0) & (to_core == core)
+
+                @pl.when(stays)
+                def _():
+                    pltpu.make_async_copy(src, back_dst, back_sem.at[part]).start()
+
+                @pl.when(jnp.logical_not(stays))
+                def _():
+                    remote(src, back_dst, back_send_sem, back_sem.at[part], k, g).start()
+
+            else:
+                remote(src, back_dst, back_send_sem, back_sem.at[part], k, g).start()
+        return carry
+
+    lax.fori_loop(0, 8, rows_back, 0)
 
     def finish(step, carry):
-        k = (part + GROUP - step) % GROUP
+        k = lax.rem(part + GROUP - step, GROUP)
         pltpu.make_async_copy(returned.at[k], returned.at[k], back_sem.at[k]).wait()
-        out_ref[:, pl.ds(pl.multiple_of(k * WIDE, WIDE), WIDE)] = nn_dot(
-            back_one_hot[...], returned[k]
-        ).astype(BF16)
         return carry
 
     lax.fori_loop(0, GROUP, finish, 0)
@@ -403,15 +449,8 @@
     pltpu.make_async_copy(most, most, send_sem).wait()
     pltpu.make_async_copy(most, most, back_send_sem).wait()
 
-    @pl.when(part == ring % 8)
-    def _():
-        fifteen = meta_out.at[pl.ds(0, RINGS - 1)]
-        pltpu.make_async_copy(fifteen, fifteen, meta_send_sem).wait()
-
-    @pl.when(part != ring % 8)
-    def _():
-        pltpu.make_async_copy(meta_out, meta_out, meta_send_sem).wait()
-
+    fifteen = meta_out.at[pl.ds(0, RINGS - 1)]
+    pltpu.make_async_copy(fifteen, fifteen, meta_send_sem).wait()
     to_next.wait_send()
     to_last.wait_send()
 
@@ -421,7 +460,7 @@
             meta.at[part], meta.at[part], spread_send_sem.at[step], spread_sem.at[part], k, ring
         ).wait_send()
         remote(
-            partial.at[k], gathered.at[part], score_send_sem.at[step], score_sem.at[part], k, ring
+            partial.at[k], gathered.at[part], score_send_sem.at[k], score_sem.at[part], k, ring
         ).wait_send()
         remote(
             weights.at[part], weights.at[part], weight_send_sem.at[step], weight_sem.at[part], k, ring
@@ -441,6 +480,12 @@
         lax.fori_loop(0, GROUP, far_wait, 0)
 
 
+def finish_kernel(loss_in, returned, back_one_hot, loss_ref, out_ref):
+    loss_ref[...] = loss_in[...]
+    for k in range(GROUP):
+        out_ref[:, k * WIDE : (k + 1) * WIDE] = nn_dot(back_one_hot[...], returned[k]).astype(BF16)
+
+
 def local(segment_sums, lengths, targets, tile_masks):
     width = segment_sums.shape[1]
     factor = 16.0 / math.sqrt(width)
@@ -448,17 +493,18 @@
     vmem = pl.BlockSpec(memory_space=pltpu.VMEM)
     smem = pl.BlockSpec(memory_space=pltpu.SMEM)
     dma = pltpu.SemaphoreType.DMA
-    losses, gradients = pl.pallas_call(
+    results = pl.pallas_call(
         functools.partial(kernel, factor, coefficient),
         out_shape=(
             jax.ShapeDtypeStruct((1, PAIRS), F32),
-            jax.ShapeDtypeStruct((ROWS, width), BF16),
+            jax.ShapeDtypeStruct((GROUP, 2 * ROWS, WIDE), BF16),
+            jax.ShapeDtypeStruct((ROWS, 2 * ROWS), BF16),
         ),
-        in_specs=[vmem, vmem, vmem, smem],
-        out_specs=(vmem, vmem),
+        in_specs=[pl.BlockSpec(memory_space=pl.ANY), vmem, vmem, smem],
+        out_specs=(vmem, vmem, vmem),
         scratch_shapes=[
+            pltpu.VMEM((ROWS, width), BF16),
             pltpu.VMEM((2 * ROWS, ROWS), BF16),
-            pltpu.VMEM((ROWS, 2 * ROWS), BF16),
             pltpu.VMEM((GROUP, 2 * ROWS, WIDE), BF16),
             pltpu.VMEM((DEVICES * MSG, WIDE), BF16),
             pltpu.VMEM((RINGS, 2, ROWS), F32),
@@ -467,6 +513,7 @@
             pltpu.VMEM((16, GROUP * ROWS, ROWS), BF16),
             pltpu.VMEM((DEVICES * MSG, GROUP * ROWS), BF16),
             pltpu.VMEM((GROUP * ROWS, ROWS), F32),
+            pltpu.VMEM((16 * PAIRS, WIDE), F32),
             pltpu.VMEM((9 * PAIRS, WIDE), BF16),
             pltpu.VMEM((9 * PAIRS, WIDE), BF16),
             pltpu.VMEM((GROUP, PAIRS, 2 * PAIRS), F32),
@@ -475,7 +522,7 @@
             pltpu.VMEM((9 * PAIRS, WIDE), F32),
             pltpu.VMEM((16 * PAIRS, WIDE), BF16),
             pltpu.VMEM((DEVICES * MSG, WIDE), BF16),
-            pltpu.VMEM((GROUP, 2 * ROWS, WIDE), BF16),
+            dma,
             dma,
             dma((GROUP,)),
             dma,
@@ -494,7 +541,16 @@
         compiler_params=pltpu.CompilerParams(
             collective_id=0, has_side_effects=True, vmem_limit_bytes=56 << 20
         ),
-    )(segment_sums, lengths.reshape(1, ROWS), targets.reshape(1, ROWS), tile_masks.reshape(8))
+    )(segment_sums, lengths.reshape(1, ROWS), targets.reshape(1, ROWS), tile_masks)
+    losses, gradients = pl.pallas_call(
+        finish_kernel,
+        out_shape=(
+            jax.ShapeDtypeStruct((1, PAIRS), F32),
+            jax.ShapeDtypeStruct((ROWS, width), BF16),
+        ),
+        in_specs=[vmem, vmem, vmem],
+        out_specs=(vmem, vmem),
+    )(*results)
     return losses.reshape(PAIRS), gradients
 
 

time: 107 us -> 86.8 us (0.81)
  the two profiles are of different devices: /device:TPU:0 before, /device:TPU:1 now
where the time goes in v2:
time: 86.8 us; the launch traced here: 86.6 us
  Pallas kernels  86 us (99%)
    pallas_call x1, Pallas kernels, local(): pl.pallas_call(functools.partial(kernel, factor, coefficient), out_shape=...  83 us
    pallas_call x1, Pallas kernels, local(): pl.pallas_call(finish_kernel, out_shape=(jax.ShapeDtypeStruct((1, PAIRS),...  3.01 us

profile of v2, /device:TPU:1, one launch (start us, length us, event | category | flops | bytes accessed | tf_op | source)
XLA Modules:
  0.0 86.6 jit_solution(17706482596245066464)
XLA Ops:
  0.6 83.0 %shard_map.59 = (f32[1,64]{1,0:T(1,128)}, bf16[8,256,512]{2,1,0:T(8,128)(2,1)}, bf16[128,256]{1,0:T(8,128)(2,1)}) custom-call(bf16[128,4096]{1,0:T(8,128)(2,1)} %sums_hbm.1, s32[1,128]{1,0:T(1,128)} %bitcast.3, s32[1,128]{1,0:T(1,128)} %bitcast.4, s32[1,2,2,2]{3,2,1,0:T(2,128)} %masks_ref.1), custom_call_target="tpu_custom_call" | custom-call | tf_op jit(solution)/shard_map/pallas_call | solution.py:496
  83.6 3.0 %shard_map.60 = (f32[1,64]{1,0:T(1,128)}, bf16[128,4096]{1,0:T(8,128)(2,1)}) custom-call(f32[1,64]{1,0:T(1,128)} %get-tuple-element.7.loss_in, bf16[8,256,512]{2,1,0:T(8,128)(2,1)} %get-tuple-element.8.returned, bf16[128,256]{1,0:T(8,128)(2,1)} %get-tuple-element.9.back_one_hot), custom_call_target="tpu_custom_call" | custom-call | tf_op jit(solution)/shard_map/pallas_call | solution.py:545

commit v3 on v2

v3 whole, which is shorter than its diff:
```python
import functools
import math

import jax
import jax.numpy as jnp
from jax import lax
from jax.experimental import pallas as pl
from jax.experimental.pallas import tpu as pltpu
from jax.sharding import PartitionSpec as P

MESH = pl.DeviceIdType.MESH
GROUP = 8
WIDE = 512
RINGS = 16
DEVICES = 128
ROWS = 128
PAIRS = 64
MSG = 16
F32 = jnp.float32
BF16 = jnp.bfloat16


def iota(shape, dim):
    return lax.broadcasted_iota(jnp.int32, shape, dim)


def nt_dot(a, b):
    return lax.dot_general(a, b, (((1,), (1,)), ((), ())), preferred_element_type=F32)


def tn_dot(a, b):
    return lax.dot_general(a, b, (((0,), (0,)), ((), ())), preferred_element_type=F32)


def nn_dot(a, b):
    return jnp.dot(a, b, preferred_element_type=F32)


def one_hot(mask):
    return jnp.where(mask, 1.0, 0.0).astype(BF16)


def place(part, ring):
    return (lax.rem(ring, 8) // 2) * 8 + part, lax.rem(ring, 2) * 2 + ring // 8


def kernel(
    factor,
    coefficient,
    sums_hbm,
    lengths_ref,
    targets_ref,
    masks_ref,
    loss_ref,
    returned,
    back_one_hot,
    sums_ref,
    send_one_hot,
    sent,
    relay,
    landed,
    meta_out,
    meta,
    codes,
    place_one_hot,
    return_one_hot,
    inverse,
    placed,
    queries,
    documents,
    partial,
    gathered,
    weights,
    gradients,
    returning,
    load_sem,
    send_sem,
    land_sem,
    meta_send_sem,
    meta_sem,
    spread_send_sem,
    spread_sem,
    side_send_sem,
    side_sem,
    score_send_sem,
    score_sem,
    weight_send_sem,
    weight_sem,
    back_send_sem,
    back_sem,
    relay_send_sem,
    relay_sem,
):
    blk = lax.axis_index("blk")
    dp = lax.axis_index("dp")
    part = lax.rem(blk, 8)
    ring = lax.rem(dp, 2) * 8 + (blk // 8) * 2 + dp // 2
    x, y = lax.rem(blk, 16) // 4, lax.rem(blk, 4)
    z, core = (dp // 2) * 2 + blk // 16, lax.rem(dp, 2)
    own_sum = lax.rem(x + y + z, 4)
    me = (own_sum * 2 + core) * 16 + x * 4 + y
    xs = [lax.rem(x + i, 4) for i in range(4)]
    ys = [lax.rem(y + j, 4) for j in range(4)]

    def class_peers(turn, to_core):
        zs = [lax.rem(z + turn + 4 - m, 4) for m in range(4)]
        zs = [lax.rem(v, 2) * 4 + v // 2 + to_core * 8 for v in zs]
        for i in range(4):
            for j in range(4):
                yield (
                    lax.rem(xs[i], 2) * 4 + ys[j],
                    (xs[i] // 2) * 2 + zs[(i + j) % 4],
                    xs[i] * 4 + ys[j],
                )

    def remote(src, dst, send, recv, to_part, to_ring):
        return pltpu.make_async_remote_copy(
            src_ref=src,
            dst_ref=dst,
            send_sem=send,
            recv_sem=recv,
            device_id=place(to_part, to_ring),
            device_id_type=MESH,
        )

    barrier = pltpu.get_barrier_semaphore()

    load = pltpu.make_async_copy(sums_hbm, sums_ref, load_sem)
    load.start()

    def greet(k, g):
        pl.semaphore_signal(barrier, inc=1, device_id=place(k, g), device_id_type=MESH)

    def greet_part(step, carry):
        k = lax.rem(part + step, GROUP)
        for g in range(RINGS):
            greet(k, g)
        return carry

    for turn in range(1, RINGS):
        greet(part, lax.rem(ring + turn, RINGS))
    lax.fori_loop(1, GROUP, greet_part, 0)

    target = targets_ref[...]
    length = lengths_ref[...].astype(F32)
    shard = target // ROWS
    slot = target % ROWS
    block = shard // 4
    to_ring = (shard % 2) * 8 + (block // 8) * 2 + (shard % 4) // 2
    of_shard = one_hot(iota((DEVICES, ROWS), 0) == shard)
    earlier = one_hot(iota((ROWS, ROWS), 0) < iota((ROWS, ROWS), 1))
    before = nn_dot(of_shard, earlier)
    rank = jnp.sum(before * of_shard.astype(F32), axis=0, keepdims=True).astype(jnp.int32)
    inner = (block % 8) * 2 + rank
    position = to_ring * MSG + inner
    send_one_hot[...] = one_hot(iota((2 * ROWS, ROWS), 0) == position)
    column = jnp.transpose(jnp.broadcast_to(position.astype(F32), (ROWS, ROWS))).astype(jnp.int32)
    lanes = iota((ROWS, ROWS), 1)
    back_one_hot[:, :ROWS] = one_hot(column == lanes)
    back_one_hot[:, ROWS:] = one_hot(column == lanes + ROWS)
    code = ((slot % 2) * PAIRS + slot // 2 + 1).astype(F32)
    mine = iota((RINGS, ROWS), 0) == to_ring
    spot = one_hot(iota((ROWS, ROWS), 0) == part * MSG + inner)
    code_rows = nt_dot(jnp.where(mine, code, 0.0).astype(BF16), spot)
    length_rows = nt_dot(jnp.where(mine, length, 0.0).astype(BF16), spot)
    for g in range(RINGS):
        meta_out[g, 0:1, :] = code_rows[g : g + 1]
        meta_out[g, 1:2, :] = length_rows[g : g + 1]
    scale = 1.0 / jnp.transpose(jnp.broadcast_to(length, (ROWS, ROWS)))
    scale = jnp.concatenate([scale] * (WIDE // ROWS), axis=1)

    def pack(k):
        columns = sums_ref[:, k * WIDE : (k + 1) * WIDE].astype(F32)
        embedded = (columns * scale).astype(BF16)
        sent[k] = nn_dot(send_one_hot[...], embedded).astype(BF16)

    load.wait()
    for k in range(GROUP):
        pack(k)

    pl.semaphore_wait(barrier, DEVICES - 1)

    meta_dst = meta.at[part, me // 8]
    pltpu.make_async_copy(meta_out.at[ring], meta_dst, meta_sem).start()
    for turn in range(1, RINGS):
        g = lax.rem(ring + turn, RINGS)
        remote(meta_out.at[g], meta_dst, meta_send_sem, meta_sem, part, g).start()

    land_dst = landed.at[pl.ds(pl.multiple_of(me * MSG, MSG), MSG)]

    mate_dst = landed.at[pl.ds(pl.multiple_of((me - core * 16) * MSG, MSG), MSG)]
    hand_over = pltpu.make_async_remote_copy(
        src_ref=sent.at[:, pl.ds(ROWS, ROWS)],
        dst_ref=relay,
        send_sem=relay_send_sem.at[0],
        recv_sem=relay_sem,
        device_id=(blk, (dp // 2) * 2 + 1 - core),
        device_id_type=MESH,
    )

    def send_class(turn, to_core, source, dst, sem, stays):
        for index, (k, g, _) in enumerate(class_peers(turn, to_core)):
            src = source(k, g)
            if index == 0:

                @pl.when(stays)
                def _():
                    pltpu.make_async_copy(src, dst, land_sem.at[own_sum]).start()

                @pl.when(jnp.logical_not(stays))
                def _():
                    remote(src, dst, sem, land_sem.at[own_sum], k, g).start()

            else:
                remote(src, dst, sem, land_sem.at[own_sum], k, g).start()

    def sent_rows(k, g):
        return sent.at[k, pl.ds(pl.multiple_of(g * MSG, MSG), MSG)]

    def relay_rows(k, g):
        return relay.at[k, pl.ds(pl.multiple_of((g - GROUP) * MSG, MSG), MSG)]

    def rows_out(turn, carry):
        send_class(turn, 0, sent_rows, land_dst, send_sem, (turn == 0) & (core == 0))
        return carry

    def rows_on(turn, carry):
        send_class(turn, 1, sent_rows, land_dst, send_sem, turn == 0)
        send_class(turn, 1, relay_rows, mate_dst, relay_send_sem.at[1], turn == 0)
        return carry

    lax.fori_loop(0, 2, rows_out, 0)

    @pl.when(core == 0)
    def _():
        hand_over.start()

    pltpu.make_async_copy(meta.at[part], meta.at[part], meta_sem).wait()

    others = [lax.rem(part + step, GROUP) for step in range(1, GROUP)]
    for k in others:
        remote(meta.at[part], meta.at[part], spread_send_sem, spread_sem, k, ring).start()

    lax.fori_loop(2, 4, rows_out, 0)

    @pl.when(core == 1)
    def _():
        hand_over.wait_recv()
        lax.fori_loop(0, 4, rows_on, 0)

    seven_meta = meta.at[pl.ds(0, GROUP - 1)]
    pltpu.make_async_copy(seven_meta, seven_meta, spread_sem).wait()
    both = meta[0]
    for k in range(1, GROUP):
        both = both + meta[k]
    codes[...] = both

    inner_shard = (iota((1, ROWS), 1) % MSG) // 2

    def full_slots(pair):
        raw = pair[0:1].astype(jnp.int32) - 1
        live = jnp.where(raw >= PAIRS, 7 * PAIRS + raw, raw) + inner_shard * PAIRS
        return jnp.where(raw >= 0, live, -1)

    def build(owners, carry):
        for q in range(4):
            full = full_slots(codes[4 * owners + q])
            place_one_hot[owners, :, q * ROWS : (q + 1) * ROWS] = one_hot(
                iota((8 * ROWS, ROWS), 0) == full
            )
        return carry

    lax.fori_loop(0, 4, build, 0)

    def build_return(a, carry):
        full = full_slots(codes[a]).astype(F32)
        down = jnp.transpose(jnp.broadcast_to(full, (ROWS, ROWS))).astype(jnp.int32)
        rows = pl.ds(pl.multiple_of(a * ROWS, ROWS), ROWS)
        for s in range(GROUP):
            return_one_hot[rows, s * ROWS : (s + 1) * ROWS] = one_hot(down == lanes + s * ROWS)
        return carry

    def build_inverse(block, carry):
        rows = pl.ds(pl.multiple_of(block * 256, 256), 256)
        total = None
        for owners in range(4):
            wide = jnp.concatenate([codes[4 * owners + q][1:2] for q in range(4)], axis=1)
            wide = jnp.broadcast_to(wide, (ROWS, 4 * ROWS)).astype(BF16)
            term = nt_dot(place_one_hot[owners, rows], wide)
            total = term if total is None else total + term
        inverse[rows] = coefficient / total
        return carry

    lax.fori_loop(0, 16, build_return, 0)
    lax.fori_loop(0, 4, build_inverse, 0)

    after = core * 8 + lax.rem(lax.rem(ring, 8) + 2, 8)
    ahead = core * 8 + lax.rem(lax.rem(ring, 8) + 6, 8)
    to_next = remote(
        documents.at[8 * PAIRS :], documents.at[:PAIRS], side_send_sem.at[0], side_sem.at[0], part, after
    )
    to_last = remote(
        queries.at[:PAIRS], queries.at[8 * PAIRS :], side_send_sem.at[1], side_sem.at[1], part, ahead
    )

    def land(step):
        owners = lax.rem(own_sum + 4 - step, 4)
        rows = pl.ds(pl.multiple_of(owners * 512, 512), 512)
        pltpu.make_async_copy(landed.at[rows], landed.at[rows], land_sem.at[owners]).wait()
        return owners, rows

    def put(now, block):
        owners, rows = now
        return nn_dot(place_one_hot[owners, block * 256 : (block + 1) * 256], landed[rows])

    first = land(0)
    for block in range(4):
        placed[block * 256 : (block + 1) * 256] = put(first, block)

    def put_more(step, carry):
        now = land(step)
        for block in range(4):
            slots = pl.ds(block * 256, 256)
            placed[slots] = placed[slots] + put(now, block)
        return carry

    lax.fori_loop(1, 3, put_more, 0)
    last = land(3)
    documents[320:576] = (placed[768:1024] + put(last, 3)).astype(BF16)
    to_next.start()
    queries[0:256] = (placed[0:256] + put(last, 0)).astype(BF16)
    to_last.start()
    queries[256:512] = (placed[256:512] + put(last, 1)).astype(BF16)
    documents[64:320] = (placed[512:768] + put(last, 2)).astype(BF16)

    def score(s):
        return nt_dot(
            queries[s * PAIRS : (s + 1) * PAIRS], documents[s * PAIRS : (s + 2) * PAIRS]
        )

    def score_out(s):
        return remote(
            partial.at[s], gathered.at[part], score_send_sem, score_sem, s, ring
        )

    for s in range(1, GROUP):
        partial[s] = score(s)
    for s in others:

        @pl.when(s != 0)
        def _():
            score_out(s).start()

    to_next.wait_recv()
    partial[0] = score(0)

    @pl.when(part != 0)
    def _():
        score_out(0).start()

    gathered[part] = partial[part]

    row = iota((PAIRS, 2 * PAIRS), 0)
    col = iota((PAIRS, 2 * PAIRS), 1)

    def tile(stop, i, j):
        return masks_ref[0, stop, i, j]

    top = jnp.where(
        col < 32,
        tile(1, 0, 0),
        jnp.where(col < 64, tile(1, 0, 1), jnp.where(col < 96, 1, tile(0, 0, 1))),
    )
    low = jnp.where(
        col < 32,
        tile(1, 1, 0),
        jnp.where(col < 64, tile(1, 1, 1), jnp.where(col < 96, tile(0, 1, 0), 1)),
    )
    live = jnp.where(row < 32, top, low) > 0
    seven_scores = gathered.at[pl.ds(0, GROUP - 1)]
    pltpu.make_async_copy(seven_scores, seven_scores, score_sem).wait()
    scores = gathered[0]
    for k in range(1, GROUP):
        scores = scores + gathered[k]
    scores = factor * scores

    masked = jnp.where(live, scores, -jnp.inf)
    highest = jnp.max(masked, axis=1, keepdims=True)
    log_total = highest + jnp.log(jnp.sum(jnp.exp(masked - highest), axis=1, keepdims=True))
    weights[part] = jnp.exp(masked - log_total).astype(BF16)

    for k in others:
        remote(weights.at[part], weights.at[part], weight_send_sem, weight_sem, k, ring).start()

    @pl.when(part == 0)
    def _():
        for k in range(GROUP):
            remote(weights.at[0], weights.at[8], weight_send_sem, weight_sem, k, ahead).start()

    diagonal = jnp.sum(jnp.where(col == row + PAIRS, scores, 0.0), axis=1, keepdims=True)
    losses = jnp.where(col == row, log_total - diagonal, 0.0)
    loss_ref[...] = jnp.sum(losses, axis=0, keepdims=True)[:, :PAIRS]
    eight_weights = weights.at[pl.ds(0, GROUP)]
    pltpu.make_async_copy(eight_weights, eight_weights, weight_sem).wait()
    to_last.wait_recv()

    def spread_scale(value):
        return jnp.concatenate([value] * (WIDE // ROWS), axis=1)

    def rows_of(s):
        return slice(s * PAIRS, (s + 1) * PAIRS)

    held = None
    for s in range(GROUP + 1):
        weight = weights[s]
        far = tn_dot(weight, queries[rows_of(s)])
        if s > 0:
            slots = rows_of(GROUP + s - 1)
            gradients[slots] = ((held + far[:PAIRS]) * spread_scale(inverse[slots])).astype(BF16)
        if s < GROUP:
            held = far[PAIRS:] - queries[rows_of(s)].astype(F32)
            own = rows_of(s)
            term = nn_dot(weight, documents[s * PAIRS : (s + 2) * PAIRS])
            term = term - documents[rows_of(s + 1)].astype(F32)
            gradients[own] = (term * spread_scale(inverse[own])).astype(BF16)

    back_dst = returned.at[part, pl.ds(pl.multiple_of(ring * MSG, MSG), MSG)]

    def back_rows(label, spot):
        return returning.at[pl.ds(pl.multiple_of((label * 16 + spot) * MSG, MSG), MSG)]

    def rows_back(step, carry):
        turn, to_core = lax.rem(step, 4), step // 4
        label = lax.rem(own_sum + turn, 4) * 2 + to_core
        rows = pl.ds(pl.multiple_of(label * 256, 256), 256)
        returning[rows] = nn_dot(return_one_hot[rows], gradients[...]).astype(BF16)
        for index, (k, g, spot) in enumerate(class_peers(turn, to_core)):
            src = back_rows(label, spot)
            if index == 0:
                stays = (turn == 0) & (to_core == core)

                @pl.when(stays)
                def _():
                    pltpu.make_async_copy(src, back_dst, back_sem.at[part]).start()

                @pl.when(jnp.logical_not(stays))
                def _():
                    remote(src, back_dst, back_send_sem, back_sem.at[part], k, g).start()

            else:
                remote(src, back_dst, back_send_sem, back_sem.at[part], k, g).start()
        return carry

    lax.fori_loop(0, 8, rows_back, 0)

    def finish(step, carry):
        k = lax.rem(part + GROUP - step, GROUP)
        pltpu.make_async_copy(returned.at[k], returned.at[k], back_sem.at[k]).wait()
        return carry

    lax.fori_loop(0, GROUP, finish, 0)

    most = landed.at[pl.ds(0, (DEVICES - 1) * MSG)]
    half = landed.at[pl.ds(0, (PAIRS - 1) * MSG)]

    @pl.when(core == 0)
    def _():
        hand_over.wait_send()
        pltpu.make_async_copy(half, half, send_sem).wait()

    @pl.when(core == 1)
    def _():
        pltpu.make_async_copy(most, most, send_sem).wait()
        pltpu.make_async_copy(half, half, relay_send_sem.at[1]).wait()

    pltpu.make_async_copy(most, most, back_send_sem).wait()
    fifteen = meta_out.at[pl.ds(0, RINGS - 1)]
    pltpu.make_async_copy(fifteen, fifteen, meta_send_sem).wait()
    to_next.wait_send()
    to_last.wait_send()

    pltpu.make_async_copy(seven_meta, seven_meta, spread_send_sem).wait()
    pltpu.make_async_copy(seven_scores, seven_scores, score_send_sem).wait()
    seven_weights = weights.at[pl.ds(0, GROUP - 1)]
    pltpu.make_async_copy(seven_weights, seven_weights, weight_send_sem).wait()

    @pl.when(part == 0)
    def _():
        pltpu.make_async_copy(eight_weights, eight_weights, weight_send_sem).wait()


def finish_kernel(loss_in, returned, back_one_hot, loss_ref, out_ref):
    loss_ref[...] = loss_in[...]
    for k in range(GROUP):
        out_ref[:, k * WIDE : (k + 1) * WIDE] = nn_dot(back_one_hot[...], returned[k]).astype(BF16)


def local(segment_sums, lengths, targets, tile_masks):
    width = segment_sums.shape[1]
    factor = 16.0 / math.sqrt(width)
    coefficient = factor / (PAIRS * DEVICES)
    vmem = pl.BlockSpec(memory_space=pltpu.VMEM)
    smem = pl.BlockSpec(memory_space=pltpu.SMEM)
    dma = pltpu.SemaphoreType.DMA
    results = pl.pallas_call(
        functools.partial(kernel, factor, coefficient),
        out_shape=(
            jax.ShapeDtypeStruct((1, PAIRS), F32),
            jax.ShapeDtypeStruct((GROUP, 2 * ROWS, WIDE), BF16),
            jax.ShapeDtypeStruct((ROWS, 2 * ROWS), BF16),
        ),
        in_specs=[pl.BlockSpec(memory_space=pl.ANY), vmem, vmem, smem],
        out_specs=(vmem, vmem, vmem),
        scratch_shapes=[
            pltpu.VMEM((ROWS, width), BF16),
            pltpu.VMEM((2 * ROWS, ROWS), BF16),
            pltpu.VMEM((GROUP, 2 * ROWS, WIDE), BF16),
            pltpu.VMEM((GROUP, ROWS, WIDE), BF16),
            pltpu.VMEM((DEVICES * MSG, WIDE), BF16),
            pltpu.VMEM((RINGS, 2, ROWS), F32),
            pltpu.VMEM((GROUP, 16, 2, ROWS), F32),
            pltpu.VMEM((16, 2, ROWS), F32),
            pltpu.VMEM((4, GROUP * ROWS, 4 * ROWS), BF16),
            pltpu.VMEM((DEVICES * MSG, GROUP * ROWS), BF16),
            pltpu.VMEM((GROUP * ROWS, ROWS), F32),
            pltpu.VMEM((16 * PAIRS, WIDE), F32),
            pltpu.VMEM((9 * PAIRS, WIDE), BF16),
            pltpu.VMEM((9 * PAIRS, WIDE), BF16),
            pltpu.VMEM((GROUP, PAIRS, 2 * PAIRS), F32),
            pltpu.VMEM((GROUP, PAIRS, 2 * PAIRS), F32),
            pltpu.VMEM((9, PAIRS, 2 * PAIRS), BF16),
            pltpu.VMEM((16 * PAIRS, WIDE), BF16),
            pltpu.VMEM((DEVICES * MSG, WIDE), BF16),
            dma,
            dma,
            dma((4,)),
            dma,
            dma,
            dma,
            dma,
            dma((2,)),
            dma((2,)),
            dma,
            dma,
            dma,
            dma,
            dma,
            dma((GROUP,)),
            dma((2,)),
            dma,
        ],
        compiler_params=pltpu.CompilerParams(
            collective_id=0, has_side_effects=True, vmem_limit_bytes=56 << 20
        ),
    )(segment_sums, lengths.reshape(1, ROWS), targets.reshape(1, ROWS), tile_masks)
    losses, gradients = pl.pallas_call(
        finish_kernel,
        out_shape=(
            jax.ShapeDtypeStruct((1, PAIRS), F32),
            jax.ShapeDtypeStruct((ROWS, width), BF16),
        ),
        in_specs=[vmem, vmem, vmem],
        out_specs=(vmem, vmem),
    )(*results)
    return losses.reshape(PAIRS), gradients


def solution(mesh):
    in_specs = (
        P(("blk", "dp"), None),
        P(("blk", "dp")),
        P(("blk", "dp")),
        P(("blk", "dp"), None, None, None),
    )
    out_specs = (P(("blk", "dp")), P(("blk", "dp"), None))
    return jax.shard_map(local, mesh=mesh, in_specs=in_specs, out_specs=out_specs, check_vma=False)
```

time: 86.8 us -> 83.2 us (0.959)
  Pallas kernels: 86 us -> 82.4 us
    pallas_call x1, Pallas kernels: 83 us -> 79.4 us  [local(): pl.pallas_call(functools.partial(kernel, factor, coefficient), out_shape=...]
where the time goes in v3:
time: 83.2 us; the launch traced here: 83 us
  Pallas kernels  82.4 us (99%)
    pallas_call x1, Pallas kernels, local(): pl.pallas_call(functools.partial(kernel, factor, coefficient), out_shape=...  79.4 us
    pallas_call x1, Pallas kernels, local(): pl.pallas_call(finish_kernel, out_shape=(jax.ShapeDtypeStruct((1, PAIRS),...  3.01 us

profile of v3, /device:TPU:1, one launch (start us, length us, event | category | flops | bytes accessed | tf_op | source)
XLA Modules:
  0.0 83.0 jit_solution(2230109661326764788)
XLA Ops:
  0.6 79.4 %shard_map.59 = (f32[1,64]{1,0:T(1,128)}, bf16[8,256,512]{2,1,0:T(8,128)(2,1)}, bf16[128,256]{1,0:T(8,128)(2,1)}) custom-call(bf16[128,4096]{1,0:T(8,128)(2,1)} %sums_hbm.1, s32[1,128]{1,0:T(1,128)} %bitcast.3, s32[1,128]{1,0:T(1,128)} %bitcast.4, s32[1,2,2,2]{3,2,1,0:T(2,128)} %masks_ref.1), custom_call_target="tpu_custom_call" | custom-call | tf_op jit(solution)/shard_map/pallas_call | solution.py:505
  80.0 3.0 %shard_map.60 = (f32[1,64]{1,0:T(1,128)}, bf16[128,4096]{1,0:T(8,128)(2,1)}) custom-call(f32[1,64]{1,0:T(1,128)} %get-tuple-element.7.loss_in, bf16[8,256,512]{2,1,0:T(8,128)(2,1)} %get-tuple-element.8.returned, bf16[128,256]{1,0:T(8,128)(2,1)} %get-tuple-element.9.back_one_hot), custom_call_target="tpu_custom_call" | custom-call | tf_op jit(solution)/shard_map/pallas_call | solution.py:556

commit v4 on v3

--- a/solution.py
+++ b/solution.py
@@ -40,8 +40,13 @@
     return jnp.where(mask, 1.0, 0.0).astype(BF16)
 
 
+def mirror(part, group):
+    return lax.rem(part // 4 + group, 2) * 4 + lax.rem(part, 4)
+
+
 def place(part, ring):
-    return (lax.rem(ring, 8) // 2) * 8 + part, lax.rem(ring, 2) * 2 + ring // 8
+    group = lax.rem(ring, 8) // 2
+    return group * 8 + mirror(part, group), lax.rem(ring, 2) * 2 + ring // 8
 
 
 def kernel(
@@ -93,7 +98,8 @@
 ):
     blk = lax.axis_index("blk")
     dp = lax.axis_index("dp")
-    part = lax.rem(blk, 8)
+    home = lax.rem(blk, 8)
+    part = mirror(home, blk // 8)
     ring = lax.rem(dp, 2) * 8 + (blk // 8) * 2 + dp // 2
     x, y = lax.rem(blk, 16) // 4, lax.rem(blk, 4)
     z, core = (dp // 2) * 2 + blk // 16, lax.rem(dp, 2)
@@ -108,7 +114,7 @@
         for i in range(4):
             for j in range(4):
                 yield (
-                    lax.rem(xs[i], 2) * 4 + ys[j],
+                    lax.rem(xs[i] + xs[i] // 2, 2) * 4 + ys[j],
                     (xs[i] // 2) * 2 + zs[(i + j) % 4],
                     xs[i] * 4 + ys[j],
                 )
@@ -160,7 +166,7 @@
     back_one_hot[:, ROWS:] = one_hot(column == lanes + ROWS)
     code = ((slot % 2) * PAIRS + slot // 2 + 1).astype(F32)
     mine = iota((RINGS, ROWS), 0) == to_ring
-    spot = one_hot(iota((ROWS, ROWS), 0) == part * MSG + inner)
+    spot = one_hot(iota((ROWS, ROWS), 0) == home * MSG + inner)
     code_rows = nt_dot(jnp.where(mine, code, 0.0).astype(BF16), spot)
     length_rows = nt_dot(jnp.where(mine, length, 0.0).astype(BF16), spot)
     for g in range(RINGS):
@@ -340,12 +346,18 @@
 
     def score_out(s):
         return remote(
-            partial.at[s], gathered.at[part], score_send_sem, score_sem, s, ring
+            partial.at[s],
+            gathered.at[part],
+            score_send_sem,
+            score_sem,
+            mirror(s, blk // 8),
+            ring,
         )
 
     for s in range(1, GROUP):
         partial[s] = score(s)
-    for s in others:
+    for k in others:
+        s = mirror(k, blk // 8)
 
         @pl.when(s != 0)
         def _():
@@ -354,11 +366,11 @@
     to_next.wait_recv()
     partial[0] = score(0)
 
-    @pl.when(part != 0)
+    @pl.when(home != 0)
     def _():
         score_out(0).start()
 
-    gathered[part] = partial[part]
+    gathered[part] = partial[home]
 
     row = iota((PAIRS, 2 * PAIRS), 0)
     col = iota((PAIRS, 2 * PAIRS), 1)
@@ -387,15 +399,15 @@
     masked = jnp.where(live, scores, -jnp.inf)
     highest = jnp.max(masked, axis=1, keepdims=True)
     log_total = highest + jnp.log(jnp.sum(jnp.exp(masked - highest), axis=1, keepdims=True))
-    weights[part] = jnp.exp(masked - log_total).astype(BF16)
-
-    for k in others:
-        remote(weights.at[part], weights.at[part], weight_send_sem, weight_sem, k, ring).start()
-
-    @pl.when(part == 0)
+    weights[home] = jnp.exp(masked - log_total).astype(BF16)
+
+    @pl.when(home == 0)
     def _():
         for k in range(GROUP):
             remote(weights.at[0], weights.at[8], weight_send_sem, weight_sem, k, ahead).start()
+
+    for k in others:
+        remote(weights.at[home], weights.at[home], weight_send_sem, weight_sem, k, ring).start()
 
     diagonal = jnp.sum(jnp.where(col == row + PAIRS, scores, 0.0), axis=1, keepdims=True)
     losses = jnp.where(col == row, log_total - diagonal, 0.0)
@@ -430,7 +442,7 @@
         return returning.at[pl.ds(pl.multiple_of((label * 16 + spot) * MSG, MSG), MSG)]
 
     def rows_back(step, carry):
-        turn, to_core = lax.rem(step, 4), step // 4
+        turn, to_core = lax.rem(step, 4), lax.rem(step // 4 + core, 2)
         label = lax.rem(own_sum + turn, 4) * 2 + to_core
         rows = pl.ds(pl.multiple_of(label * 256, 256), 256)
         returning[rows] = nn_dot(return_one_hot[rows], gradients[...]).astype(BF16)
@@ -484,7 +496,7 @@
     seven_weights = weights.at[pl.ds(0, GROUP - 1)]
     pltpu.make_async_copy(seven_weights, seven_weights, weight_send_sem).wait()
 
-    @pl.when(part == 0)
+    @pl.when(home == 0)
     def _():
         pltpu.make_async_copy(eight_weights, eight_weights, weight_send_sem).wait()
 

time: 83.2 us -> 81 us (0.974)
  the two profiles are of different devices: /device:TPU:1 before, /device:TPU:0 now
where the time goes in v4:
time: 81 us; the launch traced here: 80.9 us
  Pallas kernels  80.2 us (99%)
    pallas_call x1, Pallas kernels, local(): pl.pallas_call(functools.partial(kernel, factor, coefficient), out_shape=...  77.2 us
    pallas_call x1, Pallas kernels, local(): pl.pallas_call(finish_kernel, out_shape=(jax.ShapeDtypeStruct((1, PAIRS),...  3.01 us

profile of v4, /device:TPU:0, one launch (start us, length us, event | category | flops | bytes accessed | tf_op | source)
XLA Modules:
  0.0 80.9 jit_solution(17142099290708234773)
XLA Ops:
  0.6 77.2 %shard_map.59 = (f32[1,64]{1,0:T(1,128)}, bf16[8,256,512]{2,1,0:T(8,128)(2,1)}, bf16[128,256]{1,0:T(8,128)(2,1)}) custom-call(bf16[128,4096]{1,0:T(8,128)(2,1)} %sums_hbm.1, s32[1,128]{1,0:T(1,128)} %bitcast.3, s32[1,128]{1,0:T(1,128)} %bitcast.4, s32[1,2,2,2]{3,2,1,0:T(2,128)} %masks_ref.1), custom_call_target="tpu_custom_call" | custom-call | tf_op jit(solution)/shard_map/pallas_call | solution.py:517
  77.9 3.0 %shard_map.60 = (f32[1,64]{1,0:T(1,128)}, bf16[128,4096]{1,0:T(8,128)(2,1)}) custom-call(f32[1,64]{1,0:T(1,128)} %get-tuple-element.7.loss_in, bf16[8,256,512]{2,1,0:T(8,128)(2,1)} %get-tuple-element.8.returned, bf16[128,256]{1,0:T(8,128)(2,1)} %get-tuple-element.9.back_one_hot), custom_call_target="tpu_custom_call" | custom-call | tf_op jit(solution)/shard_map/pallas_call | solution.py:568

commit v5 on v4

--- a/solution.py
+++ b/solution.py
@@ -91,6 +91,8 @@
     score_sem,
     weight_send_sem,
     weight_sem,
+    far_send_sem,
+    far_sem,
     back_send_sem,
     back_sem,
     relay_send_sem,
@@ -398,23 +400,24 @@
 
     masked = jnp.where(live, scores, -jnp.inf)
     highest = jnp.max(masked, axis=1, keepdims=True)
-    log_total = highest + jnp.log(jnp.sum(jnp.exp(masked - highest), axis=1, keepdims=True))
-    weights[home] = jnp.exp(masked - log_total).astype(BF16)
+    shares = jnp.exp(masked - highest)
+    share_total = jnp.sum(shares, axis=1, keepdims=True)
+    weights[home] = (shares * (1.0 / share_total)).astype(BF16)
 
     @pl.when(home == 0)
     def _():
         for k in range(GROUP):
-            remote(weights.at[0], weights.at[8], weight_send_sem, weight_sem, k, ahead).start()
+            remote(weights.at[0], weights.at[8], far_send_sem, far_sem, k, ahead).start()
 
     for k in others:
         remote(weights.at[home], weights.at[home], weight_send_sem, weight_sem, k, ring).start()
 
+    log_total = highest + jnp.log(share_total)
     diagonal = jnp.sum(jnp.where(col == row + PAIRS, scores, 0.0), axis=1, keepdims=True)
     losses = jnp.where(col == row, log_total - diagonal, 0.0)
     loss_ref[...] = jnp.sum(losses, axis=0, keepdims=True)[:, :PAIRS]
-    eight_weights = weights.at[pl.ds(0, GROUP)]
-    pltpu.make_async_copy(eight_weights, eight_weights, weight_sem).wait()
-    to_last.wait_recv()
+    seven_weights = weights.at[pl.ds(0, GROUP - 1)]
+    pltpu.make_async_copy(seven_weights, seven_weights, weight_sem).wait()
 
     def spread_scale(value):
         return jnp.concatenate([value] * (WIDE // ROWS), axis=1)
@@ -424,6 +427,9 @@
 
     held = None
     for s in range(GROUP + 1):
+        if s == GROUP:
+            to_last.wait_recv()
+            pltpu.make_async_copy(weights.at[s], weights.at[s], far_sem).wait()
         weight = weights[s]
         far = tn_dot(weight, queries[rows_of(s)])
         if s > 0:
@@ -493,12 +499,12 @@
 
     pltpu.make_async_copy(seven_meta, seven_meta, spread_send_sem).wait()
     pltpu.make_async_copy(seven_scores, seven_scores, score_send_sem).wait()
-    seven_weights = weights.at[pl.ds(0, GROUP - 1)]
     pltpu.make_async_copy(seven_weights, seven_weights, weight_send_sem).wait()
 
     @pl.when(home == 0)
     def _():
-        pltpu.make_async_copy(eight_weights, eight_weights, weight_send_sem).wait()
+        eight_weights = weights.at[pl.ds(0, GROUP)]
+        pltpu.make_async_copy(eight_weights, eight_weights, far_send_sem).wait()
 
 
 def finish_kernel(loss_in, returned, back_one_hot, loss_ref, out_ref):
@@ -557,6 +563,8 @@
             dma,
             dma,
             dma,
+            dma,
+            dma,
             dma((GROUP,)),
             dma((2,)),
             dma,

time: 81 us -> 80.9 us (level)
  no operation moved by 1% of the time
where the time goes in v5:
time: 80.9 us; the launch traced here: 80.7 us
  Pallas kernels  80.1 us (99%)
    pallas_call x1, Pallas kernels, local(): pl.pallas_call(functools.partial(kernel, factor, coefficient), out_shape=...  77.1 us
    pallas_call x1, Pallas kernels, local(): pl.pallas_call(finish_kernel, out_shape=(jax.ShapeDtypeStruct((1, PAIRS),...  3.01 us

profile of v5, /device:TPU:0, one launch (start us, length us, event | category | flops | bytes accessed | tf_op | source)
XLA Modules:
  0.0 80.7 jit_solution(8459610813213381036)
XLA Ops:
  0.6 77.1 %shard_map.59 = (f32[1,64]{1,0:T(1,128)}, bf16[8,256,512]{2,1,0:T(8,128)(2,1)}, bf16[128,256]{1,0:T(8,128)(2,1)}) custom-call(bf16[128,4096]{1,0:T(8,128)(2,1)} %sums_hbm.1, s32[1,128]{1,0:T(1,128)} %bitcast.3, s32[1,128]{1,0:T(1,128)} %bitcast.4, s32[1,2,2,2]{3,2,1,0:T(2,128)} %masks_ref.1), custom_call_target="tpu_custom_call" | custom-call | tf_op jit(solution)/shard_map/pallas_call | solution.py:523
  77.7 3.0 %shard_map.60 = (f32[1,64]{1,0:T(1,128)}, bf16[128,4096]{1,0:T(8,128)(2,1)}) custom-call(f32[1,64]{1,0:T(1,128)} %get-tuple-element.7.loss_in, bf16[8,256,512]{2,1,0:T(8,128)(2,1)} %get-tuple-element.8.returned, bf16[128,256]{1,0:T(8,128)(2,1)} %get-tuple-element.9.back_one_hot), custom_call_target="tpu_custom_call" | custom-call | tf_op jit(solution)/shard_map/pallas_call | solution.py:576

commit v6 on v5

--- a/solution.py
+++ b/solution.py
@@ -57,6 +57,7 @@
     targets_ref,
     masks_ref,
     loss_ref,
+    out_ref,
     returned,
     back_one_hot,
     sums_ref,
@@ -180,7 +181,8 @@
     def pack(k):
         columns = sums_ref[:, k * WIDE : (k + 1) * WIDE].astype(F32)
         embedded = (columns * scale).astype(BF16)
-        sent[k] = nn_dot(send_one_hot[...], embedded).astype(BF16)
+        sums_ref[:, k * WIDE : (k + 1) * WIDE] = embedded
+        sent[k, :ROWS] = nn_dot(send_one_hot[:ROWS], embedded).astype(BF16)
 
     load.wait()
     for k in range(GROUP):
@@ -238,6 +240,10 @@
         return carry
 
     lax.fori_loop(0, 2, rows_out, 0)
+
+    for k in range(GROUP):
+        embedded = sums_ref[:, k * WIDE : (k + 1) * WIDE]
+        sent[k, ROWS:] = nn_dot(send_one_hot[ROWS:], embedded).astype(BF16)
 
     @pl.when(core == 0)
     def _():
@@ -474,6 +480,9 @@
     def finish(step, carry):
         k = lax.rem(part + GROUP - step, GROUP)
         pltpu.make_async_copy(returned.at[k], returned.at[k], back_sem.at[k]).wait()
+        out_ref[:, pl.ds(pl.multiple_of(k * WIDE, WIDE), WIDE)] = nn_dot(
+            back_one_hot[...], returned[k]
+        ).astype(BF16)
         return carry
 
     lax.fori_loop(0, GROUP, finish, 0)
@@ -507,10 +516,9 @@
         pltpu.make_async_copy(eight_weights, eight_weights, far_send_sem).wait()
 
 
-def finish_kernel(loss_in, returned, back_one_hot, loss_ref, out_ref):
+def finish_kernel(loss_in, rows_in, loss_ref, out_ref):
     loss_ref[...] = loss_in[...]
-    for k in range(GROUP):
-        out_ref[:, k * WIDE : (k + 1) * WIDE] = nn_dot(back_one_hot[...], returned[k]).astype(BF16)
+    out_ref[...] = rows_in[...]
 
 
 def local(segment_sums, lengths, targets, tile_masks):
@@ -524,12 +532,13 @@
         functools.partial(kernel, factor, coefficient),
         out_shape=(
             jax.ShapeDtypeStruct((1, PAIRS), F32),
-            jax.ShapeDtypeStruct((GROUP, 2 * ROWS, WIDE), BF16),
-            jax.ShapeDtypeStruct((ROWS, 2 * ROWS), BF16),
+            jax.ShapeDtypeStruct((ROWS, width), BF16),
         ),
         in_specs=[pl.BlockSpec(memory_space=pl.ANY), vmem, vmem, smem],
-        out_specs=(vmem, vmem, vmem),
+        out_specs=(vmem, vmem),
         scratch_shapes=[
+            pltpu.VMEM((GROUP, 2 * ROWS, WIDE), BF16),
+            pltpu.VMEM((ROWS, 2 * ROWS), BF16),
             pltpu.VMEM((ROWS, width), BF16),
             pltpu.VMEM((2 * ROWS, ROWS), BF16),
             pltpu.VMEM((GROUP, 2 * ROWS, WIDE), BF16),
@@ -579,7 +588,7 @@
             jax.ShapeDtypeStruct((1, PAIRS), F32),
             jax.ShapeDtypeStruct((ROWS, width), BF16),
         ),
-        in_specs=[vmem, vmem, vmem],
+        in_specs=[vmem, vmem],
         out_specs=(vmem, vmem),
     )(*results)
     return losses.reshape(PAIRS), gradients

time: 80.9 us -> 80.9 us (level)
  no operation moved by 1% of the time
where the time goes in v6:
time: 80.9 us; the launch traced here: 80.7 us
  Pallas kernels  80.1 us (99%)
    pallas_call x1, Pallas kernels, local(): pl.pallas_call(functools.partial(kernel, factor, coefficient), out_shape=...  77.8 us
    pallas_call x1, Pallas kernels, local(): pl.pallas_call(finish_kernel, out_shape=(jax.ShapeDtypeStruct((1, PAIRS),...  2.27 us

profile of v6, /device:TPU:0, one launch (start us, length us, event | category | flops | bytes accessed | tf_op | source)
XLA Modules:
  0.0 80.7 jit_solution(17467663157774406365)
XLA Ops:
  0.6 77.8 %shard_map.59 = (f32[1,64]{1,0:T(1,128)}, bf16[128,4096]{1,0:T(8,128)(2,1)}) custom-call(bf16[128,4096]{1,0:T(8,128)(2,1)} %sums_hbm.1, s32[1,128]{1,0:T(1,128)} %bitcast.3, s32[1,128]{1,0:T(1,128)} %bitcast.4, s32[1,2,2,2]{3,2,1,0:T(2,128)} %masks_ref.1), custom_call_target="tpu_custom_call" | custom-call | tf_op jit(solution)/shard_map/pallas_call | solution.py:531
  78.5 2.3 %shard_map.60 = (f32[1,64]{1,0:T(1,128)}, bf16[128,4096]{1,0:T(8,128)(2,1)}) custom-call(f32[1,64]{1,0:T(1,128)} %get-tuple-element.6.loss_in, bf16[128,4096]{1,0:T(8,128)(2,1)} %get-tuple-element.7.rows_in), custom_call_target="tpu_custom_call" | custom-call | tf_op jit(solution)/shard_map/pallas_call | solution.py:585

commit v7 on v5

--- a/solution.py
+++ b/solution.py
@@ -147,7 +147,8 @@
 
     for turn in range(1, RINGS):
         greet(part, lax.rem(ring + turn, RINGS))
-    lax.fori_loop(1, GROUP, greet_part, 0)
+    for step in range(1, GROUP):
+        greet_part(step, 0)
 
     target = targets_ref[...]
     length = lengths_ref[...].astype(F32)

time: 80.9 us -> 80.9 us (level)
  no operation moved by 1% of the time
where the time goes in v7:
time: 80.9 us; the launch traced here: 80.7 us
  Pallas kernels  80.1 us (99%)
    pallas_call x1, Pallas kernels, local(): pl.pallas_call(functools.partial(kernel, factor, coefficient), out_shape=...  77.1 us
    pallas_call x1, Pallas kernels, local(): pl.pallas_call(finish_kernel, out_shape=(jax.ShapeDtypeStruct((1, PAIRS),...  3.01 us

profile of v7, /device:TPU:0, one launch (start us, length us, event | category | flops | bytes accessed | tf_op | source)
XLA Modules:
  0.0 80.7 jit_solution(9249021616825462318)
XLA Ops:
  0.6 77.1 %shard_map.59 = (f32[1,64]{1,0:T(1,128)}, bf16[8,256,512]{2,1,0:T(8,128)(2,1)}, bf16[128,256]{1,0:T(8,128)(2,1)}) custom-call(bf16[128,4096]{1,0:T(8,128)(2,1)} %sums_hbm.1, s32[1,128]{1,0:T(1,128)} %bitcast.3, s32[1,128]{1,0:T(1,128)} %bitcast.4, s32[1,2,2,2]{3,2,1,0:T(2,128)} %masks_ref.1), custom_call_target="tpu_custom_call" | custom-call | tf_op jit(solution)/shard_map/pallas_call | solution.py:524
  77.7 3.0 %shard_map.60 = (f32[1,64]{1,0:T(1,128)}, bf16[128,4096]{1,0:T(8,128)(2,1)}) custom-call(f32[1,64]{1,0:T(1,128)} %get-tuple-element.7.loss_in, bf16[8,256,512]{2,1,0:T(8,128)(2,1)} %get-tuple-element.8.returned, bf16[128,256]{1,0:T(8,128)(2,1)} %get-tuple-element.9.back_one_hot), custom_call_target="tpu_custom_call" | custom-call | tf_op jit(solution)/shard_map/pallas_call | solution.py:577
